TPU v7x, 256 devices: a whole 4x4x8 slice. The times are simulated.
256 devices in a mesh: blk: 8 (over z), fft: 32 (over x, y, core).
Axes of the slice: x: 4, y: 4, z: 8, core: 2. Of those that a mesh axis runs over, the one named last changes fastest.
Arguments:
- tokens: bfloat16 [32768, 1024], P(('blk', 'fft')), may hold values from -6 to 6
- w_in: bfloat16 [1024, 1536], replicated, may hold values from -0.1875 to 0.1875
- conv_taps: float32 [3, 1536], replicated, may hold values from -3 to 3
- causal_taps: bfloat16 [32768, 512], P(('blk', 'fft')), may hold values from -0.0625 to 0.0625
- anticausal_taps: bfloat16 [32768, 512], P(('blk', 'fft')), may hold values from -0.0625 to 0.0625
- skip_gain: float32 [512], replicated, may hold values from 0.1 to 1.9
- w_out: bfloat16 [512, 1024], replicated, may hold values from -0.25 to 0.25
Outputs:
- mixed_out: bfloat16 [32768, 1024], P(('blk', 'fft'))
All inputs are finite; a program needn't handle non-finite values.
Results may differ from a plain program's by a relative error of at most 0.013.
Values may be sent and summed in bfloat16 or wider, within the bound.
No kernel may reach another device: no remote copies, remote signals or barrier semaphores. Data moves between devices by JAX's collectives and lax.ppermute only.
A program may use at most 64 MiB of HBM per device.

v0:
```python
import math

import jax
import jax.numpy as jnp
import numpy as np
from jax import lax
from jax.experimental import pallas as pl
from jax.experimental.pallas import tpu as pltpu
from jax.sharding import PartitionSpec as P

AXES = ("blk", "fft")
F32 = jnp.float32
BF16 = jnp.bfloat16


def tables(blocks, tok):
    length = 2 * blocks * tok
    half = np.arange(blocks) + 0.5
    ang = 2 * math.pi * np.outer(half, np.arange(2 * blocks)) / (2 * blocks)
    fore = np.concatenate([np.cos(ang), -np.sin(ang)], 0)
    back = np.concatenate([fore[:blocks, :blocks].T, fore[blocks:, :blocks].T], 1) * (2 / length)
    fore[:, blocks:] *= -1
    twist = 2 * math.pi * np.outer(half, np.arange(tok)) / length
    inner = 2 * math.pi * np.outer(np.arange(tok), np.arange(tok)) / tok
    c, s = np.cos(inner), np.sin(inner)
    q_fore = np.block([[c, -s], [s, c]])
    q_back = np.block([[c, s], [-s, c]])
    small = [jnp.asarray(a, BF16) for a in (fore, q_fore, q_back, back)]
    return small + [jnp.asarray(np.cos(twist), F32), jnp.asarray(np.sin(twist), F32)]


def dot(a, b):
    return jnp.dot(a, b, preferred_element_type=F32)


def filter_kernel(causal_ref, anti_ref, out_ref, buf, wide):
    channels = causal_ref.shape[1]
    half = channels // 2
    for a, ref in enumerate((causal_ref, anti_ref)):
        buf[...] = ref[...].astype(F32).T
        for c in range(2):
            wide[pl.ds(2 * a + c, half, stride=4), :] = buf[pl.ds(c, half, stride=2), :]
    out_ref[...] = wide[...].astype(BF16)


def front_kernel(proj_ref, edge_ref, taps_ref, skip_ref, sig_ref, second_ref, direct_ref):
    rows = proj_ref.shape[0]
    channels = proj_ref.shape[1] // 3
    row = lax.broadcasted_iota(jnp.int32, (rows, channels), 0)

    def short(i):
        cols = slice(i * channels, (i + 1) * channels)
        mid = proj_ref[:, cols].astype(F32)
        edge = edge_ref[:, cols].astype(F32)
        up = jnp.where(row == 0, edge[0:1], pltpu.roll(mid, 1, 0))
        down = jnp.where(row == rows - 1, edge[1:2], pltpu.roll(mid, rows - 1, 0))
        return taps_ref[0:1, cols] * up + taps_ref[1:2, cols] * mid + taps_ref[2:3, cols] * down

    signal = short(0) * short(2)
    sig_ref[...] = signal.T.astype(BF16)
    second_ref[...] = short(1).T
    direct_ref[...] = (skip_ref[...] * signal).T


def conv_kernel(sig_ref, filt_ref, fore_ref, qf_ref, qb_ref, back_ref, cos_ref, sin_ref, out_ref, buf, wide):
    blocks = sig_ref.shape[0] // 2
    tok = sig_ref.shape[1]
    cos, sin = cos_ref[...], sin_ref[...]

    def spectrum(b):
        parts = []
        for c in range(2):
            lanes = slice(c * tok, (c + 1) * tok)
            re, im = b[:blocks, lanes], b[blocks:, lanes]
            parts.append(jnp.concatenate([re * cos + im * sin, im * cos - re * sin], 1))
        return dot(jnp.concatenate(parts, 0).astype(BF16), qf_ref[...])

    wide[...] = filt_ref[...].astype(F32)
    taps = [
        jnp.concatenate([wide[pl.ds(2 * a + c, blocks, stride=4), :] for c in range(2)], 1)
        for a in range(2)
    ]
    place = lax.broadcasted_iota(jnp.int32, (blocks, 2 * tok), 0)
    lane = lax.broadcasted_iota(jnp.int32, (blocks, 2 * tok), 1)
    taps[1] = jnp.where((place == 0) & (lane % tok == 0), 0.0, taps[1])
    f = spectrum(dot(fore_ref[...], jnp.concatenate(taps, 0).astype(BF16)))

    buf[...] = sig_ref[...].astype(F32)
    x = jnp.concatenate([buf[pl.ds(c, blocks, stride=2), :] for c in range(2)], 1)
    s = spectrum(dot(fore_ref[:, :blocks], x.astype(BF16)))

    sr, si, fr, fi = s[:, :tok], s[:, tok:], f[:, :tok], f[:, tok:]
    y = jnp.concatenate([sr * fr - si * fi, sr * fi + si * fr], 1)
    g = dot(y.astype(BF16), qb_ref[...])
    parts = []
    for c in range(2):
        re, im = g[c * blocks : (c + 1) * blocks, :tok], g[c * blocks : (c + 1) * blocks, tok:]
        parts.append(jnp.concatenate([re * cos - im * sin, re * sin + im * cos], 0))
    out = dot(back_ref[...], jnp.concatenate(parts, 1).astype(BF16))
    for c in range(2):
        buf[pl.ds(c, blocks, stride=2), :] = out[:, c * tok : (c + 1) * tok]
    out_ref[...] = buf[...].astype(BF16)


def last_kernel(conv_ref, second_ref, direct_ref, w_ref, out_ref):
    gated = (second_ref[...] * (conv_ref[...].astype(F32) + direct_ref[...])).astype(BF16)
    out_ref[...] = lax.dot_general(
        gated, w_ref[...], (((0,), (0,)), ((), ())), preferred_element_type=F32
    ).astype(BF16)


def call(kernel, outs, scratch=()):
    many = isinstance(outs, (list, tuple))
    return pl.pallas_call(
        kernel,
        out_shape=outs,
        scratch_shapes=list(scratch),
        compiler_params=pltpu.CompilerParams(vmem_limit_bytes=40 * 1024 * 1024),
    )


def exchange(x):
    return lax.all_to_all(x, AXES, split_axis=0, concat_axis=0, tiled=True)


def body(tokens, w_in, conv_taps, causal_taps, anticausal_taps, skip_gain, w_out):
    rows = tokens.shape[0]
    channels, width = w_out.shape
    count = lax.axis_size(AXES)
    shape = jax.ShapeDtypeStruct
    vmem = pltpu.VMEM

    filt = call(
        filter_kernel,
        shape((2 * channels, rows), BF16),
        [vmem((channels, rows), F32), vmem((2 * channels, rows), F32)],
    )(causal_taps, anticausal_taps)
    filt = exchange(filt)

    before = lax.ppermute(tokens[-1:], AXES, [(i, i + 1) for i in range(count - 1)])
    after = lax.ppermute(tokens[:1], AXES, [(i + 1, i) for i in range(count - 1)])
    proj = dot(tokens, w_in).astype(BF16)
    edge = dot(jnp.concatenate([before, after], 0), w_in).astype(BF16)
    sig, second, direct = call(
        front_kernel,
        [shape((channels, rows), BF16), shape((channels, rows), F32), shape((channels, rows), F32)],
    )(proj, edge, conv_taps, skip_gain[None])
    sig = exchange(sig)

    conv = call(
        conv_kernel,
        shape((channels, rows), BF16),
        [vmem((channels, rows), F32), vmem((2 * channels, rows), F32)],
    )(sig, filt, *tables(count, rows))
    conv = exchange(conv)
    return call(last_kernel, shape((rows, width), BF16))(conv, second, direct, w_out)


def solution(mesh):
    rows = P(AXES, None)
    in_specs = (rows, P(), P(), rows, rows, P(), P())
    return jax.shard_map(body, mesh=mesh, in_specs=in_specs, out_specs=rows, check_vma=False)
```

profile of v0, /device:TPU:1, one launch (start us, length us, event | category | flops | bytes accessed | tf_op | source)
XLA Modules:
  0.0 93.5 jit_solution(8614887594576183894)
XLA Ops:
  0.0 0.0 copy-start
  0.0 0.9 fusion.4
  0.9 4.7 %collective-permute-start = (bf16[1,1024]{1,0:T(2,128)(2,1)S(1)}, bf16[1,1024]{1,0:T(2,128)(2,1)S(1)}, u32[]{:S(2)}, u32[]{:S(2)}) collective-permute-start(bf16[1,1024]{1,0:T(2,128)(2,1)S(1)} %get-tuple-element.11), channel_id=1, source_target_pairs={{0,1},{1,2},{2,3},{3,4},{4,5},{5,6},{6,7},{7,8},{8,9},{9,10},{10,1... | collective-permute-start | bytes 6152 | tf_op jit(solution)/shard_map/ppermute | solution.py:140
  5.6 0.0 copy-start.14
  5.6 0.0 copy-start.15
  5.7 1.9 %collective-permute-start.1 = (bf16[1,1024]{1,0:T(2,128)(2,1)S(1)}, bf16[1,1024]{1,0:T(2,128)(2,1)S(1)}, u32[]{:S(2)}, u32[]{:S(2)}) collective-permute-start(bf16[1,1024]{1,0:T(2,128)(2,1)S(1)} %get-tuple-element.12), channel_id=1, source_target_pairs={{1,0},{2,1},{3,2},{4,3},{5,4},{6,5},{7,6},{8,7},{9,8},{10,9},{11,1... | collective-permute-start | bytes 6152 | tf_op jit(solution)/shard_map/ppermute | solution.py:141
  7.6 0.0 copy-done
  7.6 1.5 %convolution_convert_fusion.proj_ref = bf16[128,1536]{1,0:T(8,128)(2,1)S(1)} fusion(bf16[128,1024]{1,0:T(8,128)(2,1)} %param.13, bf16[1024,1536]{1,0:T(8,128)(2,1)S(1)} %copy-done), kind=kOutput, calls=%fused_computation | convolution fusion | flops 402849792 | bytes 3801088 | tf_op jit(solution)/shard_map/dot_general | solution.py:33
  9.1 0.0 collective-permute-done
  9.2 1.4 %collective-permute-done.1 = bf16[1,1024]{1,0:T(2,128)(2,1)S(1)} collective-permute-done((bf16[1,1024]{1,0:T(2,128)(2,1)S(1)}, bf16[1,1024]{1,0:T(2,128)(2,1)S(1)}, u32[]{:S(2)}, u32[]{:S(2)}) %collective-permute-start.1) | collective-permute-done | bytes 2080 | tf_op jit(solution)/shard_map/ppermute | solution.py:141
  10.6 0.5 convolution_convert_fusion.1.edge_ref
  11.1 0.0 copy-done.14
  11.1 0.0 copy-done.15
  11.1 1.0 %shard_map.127 = (bf16[512,128]{1,0:T(8,128)(2,1)}, f32[512,128]{1,0:T(8,128)S(1)}, f32[512,128]{1,0:T(8,128)S(1)}) custom-call(bf16[128,1536]{1,0:T(8,128)(2,1)S(1)} %convolution_convert_fusion.proj_ref, bf16[2,1536]{1,0:T(2,128)(2,1)S(1)} %convolution_convert_fusion.1.edge_ref, f32[3,1536]{1,0:T(4,128)S(1)} %copy-done.14, f32[1,512]{1,0:T(1,128)S(1)} %bitcast.15), custom_call_target="tpu_custom_call" | custom-call | tf_op jit(solution)/shard_map/pallas_call | solution.py:144
  12.1 0.0 copy-start.4
  12.1 0.7 copy-done.4
  12.8 0.0 copy-start.6
  12.8 0.7 copy-done.6
  13.5 17.8 %all-to-all-start = ((bf16[256,2,128]{2,1,0:T(2,128)(2,1)}), bf16[256,2,128]{2,1,0:T(2,128)(2,1)S(1)}, u32[]{:S(2)}, u32[]{:S(2)}) async-start(bf16[256,2,128]{2,1,0:T(2,128)(2,1)} %bitcast.1), calls=%async_computation | async-start | bytes 262144 | tf_op jit(solution)/shard_map/all_to_all | solution.py:123
  31.3 0.0 copy-start.12
  31.3 0.9 copy-done.12
  32.2 0.0 copy-start.13
  32.2 0.9 copy-done.13
  33.1 0.2 shard_map.128
  33.3 11.0 %all-to-all-done = bf16[256,2,128]{2,1,0:T(2,128)(2,1)S(1)} async-done(((bf16[256,2,128]{2,1,0:T(2,128)(2,1)}), bf16[256,2,128]{2,1,0:T(2,128)(2,1)S(1)}, u32[]{:S(2)}, u32[]{:S(2)}) %all-to-all-start) | async-done | bytes 131104 | tf_op jit(solution)/shard_map/all_to_all | solution.py:123
  44.3 0.0 copy-start.1
  44.3 20.7 %all_to_all.33 = bf16[256,4,128]{2,1,0:T(4,128)(2,1)S(1)} all-to-all(bf16[256,4,128]{2,1,0:T(4,128)(2,1)S(1)} %bitcast.11), channel_id=1, replica_groups=mesh['blk'=8,'fft'=32] {'blk','fft'}, dimensions={0} | all-to-all | bytes 524288 | tf_op jit(solution)/shard_map/all_to_all | solution.py:123
  65.0 0.0 copy-start.2
  65.0 1.0 %copy-done.2 = bf16[512,512]{1,0:T(8,128)(2,1)S(1)} copy-done((bf16[512,512]{1,0:T(8,128)(2,1)S(1)}, bf16[512,512]{1,0:T(8,128)(2,1)}, u32[]{:S(2)}) %copy-start.2) | copy-done | bytes 524312
  66.0 0.0 copy-start.3
  66.0 0.9 %copy-done.3 = bf16[256,512]{1,0:T(8,128)(2,1)S(1)} copy-done((bf16[256,512]{1,0:T(8,128)(2,1)S(1)}, bf16[256,512]{1,0:T(8,128)(2,1)}, u32[]{:S(2)}) %copy-start.3) | copy-done | bytes 262168
  66.9 0.0 copy-start.8
  66.9 0.9 copy-done.8
  67.8 0.0 copy-start.9
  67.9 0.9 copy-done.9
  68.8 0.0 copy-start.10
  68.8 0.9 copy-done.10
  69.7 0.0 copy-start.11
  69.7 0.9 copy-done.11
  70.6 1.3 %shard_map.129 = bf16[512,128]{1,0:T(8,128)(2,1)S(1)} custom-call(bf16[512,128]{1,0:T(8,128)(2,1)S(1)} %bitcast.12, bf16[1024,128]{1,0:T(8,128)(2,1)S(1)} %bitcast.10, bf16[512,512]{1,0:T(8,128)(2,1)S(1)} %copy-done.2, bf16[256,256]{1,0:T(8,128)(2,1)S(1)} %copy-done.8, bf16[256,256]{1,0:T(8,128)(2,1)S(1)} %copy-done.9, bf16[256,512]{1,0:T(8,128)(2,1)S(1)} %copy-done.3, ...), custom_call_target="tpu_custom_call" | custom-call | tf_op jit(solution)/shard_map/pallas_call | solution.py:150
  71.9 18.6 %all_to_all.34 = bf16[256,2,128]{2,1,0:T(2,128)(2,1)S(1)} all-to-all(bf16[256,2,128]{2,1,0:T(2,128)(2,1)S(1)} %bitcast.13), channel_id=1, replica_groups=mesh['blk'=8,'fft'=32] {'blk','fft'}, dimensions={0} | all-to-all | bytes 262144 | tf_op jit(solution)/shard_map/all_to_all | solution.py:123
  90.5 0.0 copy-done.1
  90.5 0.0 copy-start.5
  90.5 0.9 %copy-done.5 = f32[512,128]{1,0:T(8,128)S(1)} copy-done((f32[512,128]{1,0:T(8,128)S(1)}, f32[512,128]{1,0:T(8,128)}, u32[]{:S(2)}) %copy-start.5) | copy-done | bytes 262168
  91.5 0.0 copy-start.7
  91.5 0.9 %copy-done.7 = f32[512,128]{1,0:T(8,128)S(1)} copy-done((f32[512,128]{1,0:T(8,128)S(1)}, f32[512,128]{1,0:T(8,128)}, u32[]{:S(2)}) %copy-start.7) | copy-done | bytes 262168
  92.4 1.0 %shard_map.130 = bf16[128,1024]{1,0:T(8,128)(2,1)} custom-call(bf16[512,128]{1,0:T(8,128)(2,1)S(1)} %bitcast.14, f32[512,128]{1,0:T(8,128)S(1)} %copy-done.5, f32[512,128]{1,0:T(8,128)S(1)} %copy-done.7, bf16[512,1024]{1,0:T(8,128)(2,1)S(1)} %copy-done.1), custom_call_target="tpu_custom_call" | custom-call | tf_op jit(solution)/shard_map/pallas_call | solution.py:156
Async XLA Ops:
  0.0 7.6 %copy-start = (bf16[1024,1536]{1,0:T(8,128)(2,1)S(1)}, bf16[1024,1536]{1,0:T(8,128)(2,1)}, u32[]{:S(2)}) copy-start(bf16[1024,1536]{1,0:T(8,128)(2,1)} %param.14) | copy-start | bytes 9437188
  0.9 8.2 %collective-permute-start = (bf16[1,1024]{1,0:T(2,128)(2,1)S(1)}, bf16[1,1024]{1,0:T(2,128)(2,1)S(1)}, u32[]{:S(2)}, u32[]{:S(2)}) collective-permute-start(bf16[1,1024]{1,0:T(2,128)(2,1)S(1)} %get-tuple-element.11), channel_id=1, source_target_pairs={{0,1},{1,2},{2,3},{3,4},{4,5},{5,6},{6,7},{7,8},{8,9},{9,10},{10,1... | collective-permute-start | bytes 6152 | tf_op jit(solution)/shard_map/ppermute | solution.py:140
  5.6 5.5 %copy-start.14 = (f32[3,1536]{1,0:T(4,128)S(1)}, f32[3,1536]{1,0:T(4,128)}, u32[]{:S(2)}) copy-start(f32[3,1536]{1,0:T(4,128)} %taps_ref.1) | copy-start | bytes 55300
  5.6 5.5 %copy-start.15 = (f32[512]{0:T(512)S(1)}, f32[512]{0:T(512)}, u32[]{:S(2)}) copy-start(f32[512]{0:T(512)} %param.18) | copy-start | bytes 6148
  5.7 4.9 %collective-permute-start.1 = (bf16[1,1024]{1,0:T(2,128)(2,1)S(1)}, bf16[1,1024]{1,0:T(2,128)(2,1)S(1)}, u32[]{:S(2)}, u32[]{:S(2)}) collective-permute-start(bf16[1,1024]{1,0:T(2,128)(2,1)S(1)} %get-tuple-element.12), channel_id=1, source_target_pairs={{1,0},{2,1},{3,2},{4,3},{5,4},{6,5},{7,6},{8,7},{9,8},{10,9},{11,1... | collective-permute-start | bytes 6152 | tf_op jit(solution)/shard_map/ppermute | solution.py:141
  12.1 0.7 copy-start.4
  12.8 0.7 copy-start.6
  13.5 30.8 %all-to-all-start = ((bf16[256,2,128]{2,1,0:T(2,128)(2,1)}), bf16[256,2,128]{2,1,0:T(2,128)(2,1)S(1)}, u32[]{:S(2)}, u32[]{:S(2)}) async-start(bf16[256,2,128]{2,1,0:T(2,128)(2,1)} %bitcast.1), calls=%async_computation | async-start | bytes 262144 | tf_op jit(solution)/shard_map/all_to_all | solution.py:123
  31.3 0.9 copy-start.12
  32.2 0.9 copy-start.13
  44.3 46.2 %copy-start.1 = (bf16[512,1024]{1,0:T(8,128)(2,1)S(1)}, bf16[512,1024]{1,0:T(8,128)(2,1)}, u32[]{:S(2)}) copy-start(bf16[512,1024]{1,0:T(8,128)(2,1)} %w_ref.1) | copy-start | bytes 3145732
  65.0 1.0 %copy-start.2 = (bf16[512,512]{1,0:T(8,128)(2,1)S(1)}, bf16[512,512]{1,0:T(8,128)(2,1)}, u32[]{:S(2)}) copy-start(bf16[512,512]{1,0:T(8,128)(2,1)} %constant.12.clone.fore_ref) | copy-start | bytes 1572868
  66.0 0.9 %copy-start.3 = (bf16[256,512]{1,0:T(8,128)(2,1)S(1)}, bf16[256,512]{1,0:T(8,128)(2,1)}, u32[]{:S(2)}) copy-start(bf16[256,512]{1,0:T(8,128)(2,1)} %constant.15.clone.back_ref) | copy-start | bytes 786436
  66.9 0.9 copy-start.8
  67.8 0.9 copy-start.9
  68.8 0.9 copy-start.10
  69.7 0.9 copy-start.11
  90.5 1.0 %copy-start.5 = (f32[512,128]{1,0:T(8,128)S(1)}, f32[512,128]{1,0:T(8,128)}, u32[]{:S(2)}) copy-start(f32[512,128]{1,0:T(8,128)} %copy-done.4) | copy-start | bytes 786436
  91.5 0.9 %copy-start.7 = (f32[512,128]{1,0:T(8,128)S(1)}, f32[512,128]{1,0:T(8,128)}, u32[]{:S(2)}) copy-start(f32[512,128]{1,0:T(8,128)} %copy-done.6) | copy-start | bytes 786436
where the time goes:
time: 94 us; the launch traced here: 93.5 us
  blocking collectives  39.3 us (42%)
  starting transfers between devices  24.5 us (26%)
  waiting for transfers between devices  12.4 us (13%)
  local copies, waits for them, and re-layouts  11.6 us (12%)
  Pallas kernels  3.55 us (4%)
  matrix products  2.04 us (2%)
    all_to_all x2, blocking collectives, exchange(): return lax.all_to_all(x, AXES, split_axis=0, concat_axis=0, tiled=True)  39.3 us
    all_to_all x1, starting transfers between devices, exchange(): return lax.all_to_all(x, AXES, split_axis=0, concat_axis=0, tiled=True)  17.8 us
    all_to_all x1, waiting for transfers between devices, exchange(): return lax.all_to_all(x, AXES, split_axis=0, concat_axis=0, tiled=True)  11 us
    unnamed x32, local copies, waits for them, and re-layouts  10.7 us
    ppermute x1, starting transfers between devices, body(): lax.ppermute(tokens[-1:], AXES, [(i, i + 1) for i in range(count - 1)])  4.73 us
    dot_general x2, matrix products, dot(): return jnp.dot(a, b, preferred_element_type=F32)  2.04 us
    ppermute x1, starting transfers between devices, body(): lax.ppermute(tokens[:1], AXES, [(i + 1, i) for i in range(count - 1)])  1.92 us
  transfers between devices with their start and end apart: 3, of which 2 were waited for; matrix products, arithmetic and copies ran while one was open for 2% of the time, Pallas kernels for 0%

commit v1 on v0

v1 whole, which is shorter than its diff:
```python
import math

import jax
import jax.numpy as jnp
import numpy as np
from jax import lax
from jax.experimental import pallas as pl
from jax.experimental.pallas import tpu as pltpu
from jax.sharding import PartitionSpec as P

AXES = ("blk", "fft")
F32 = jnp.float32
BF16 = jnp.bfloat16


def tables(blocks, tok):
    length = 2 * blocks * tok
    half = np.arange(blocks) + 0.5
    ang = 2 * math.pi * np.outer(half, np.arange(2 * blocks)) / (2 * blocks)
    fore = np.concatenate([np.cos(ang), -np.sin(ang)], 0)
    back = np.concatenate([fore[:blocks, :blocks].T, fore[blocks:, :blocks].T], 0) * (2 / length)
    fore[:, blocks:] *= -1
    twist = 2 * math.pi * np.outer(half, np.arange(tok)) / length
    inner = 2 * math.pi * np.outer(np.arange(tok), np.arange(tok)) / tok
    c, s = np.cos(inner), np.sin(inner)
    inner = np.block([[c, -s], [s, c], [c, s], [-s, c]])
    return (
        jnp.asarray(np.concatenate([fore, inner, back], 1), BF16),
        jnp.asarray(np.concatenate([np.cos(twist), np.sin(twist)], 1), F32),
    )


def dot(a, b):
    return jnp.dot(a, b, preferred_element_type=F32)


def front_kernel(
    tok_ref, before_ref, after_ref, w_ref, taps_ref, skip_ref, causal_ref, anti_ref, table_ref, twist_ref,
    send_ref, second_ref, direct_ref, table_out, twist_out, buf, wide, sems,
):
    copies = [
        pltpu.make_async_copy(table_ref, table_out, sems.at[0]),
        pltpu.make_async_copy(twist_ref, twist_out, sems.at[1]),
    ]
    for copy in copies:
        copy.start()
    rows = tok_ref.shape[0]
    channels = causal_ref.shape[1]
    half = channels // 2
    row = lax.broadcasted_iota(jnp.int32, (rows, channels), 0)
    tok = jnp.concatenate([tok_ref[...], before_ref[...], after_ref[...]], 0)

    def short(i):
        cols = slice(i * channels, (i + 1) * channels)
        proj = dot(tok, w_ref[:, cols]).astype(BF16).astype(F32)
        mid = proj[:rows]
        up = jnp.where(row == 0, proj[rows + 7 : rows + 8], pltpu.roll(mid, 1, 0))
        down = jnp.where(row == rows - 1, proj[rows + 8 : rows + 9], pltpu.roll(mid, rows - 1, 0))
        return taps_ref[0:1, cols] * up + taps_ref[1:2, cols] * mid + taps_ref[2:3, cols] * down

    def place(a, block):
        buf[...] = block.T
        for c in range(2):
            wide[pl.ds(2 * a + c, half, stride=6), :] = buf[pl.ds(c, half, stride=2), :]

    place(1, causal_ref[...].astype(F32))
    place(2, anti_ref[...].astype(F32))
    signal = short(0) * short(2)
    place(0, signal)
    send_ref[...] = wide[...].astype(BF16)
    second_ref[...] = short(1).T
    direct_ref[...] = (skip_ref[...] * signal).T
    for copy in copies:
        copy.wait()


def conv_kernel(got_ref, table_ref, twist_ref, out_ref, buf, wide):
    tok = got_ref.shape[1]
    blocks = got_ref.shape[0] // 6
    cos, sin = twist_ref[:, :tok], twist_ref[:, tok:]
    inner = slice(2 * blocks, 2 * blocks + 2 * tok)
    back = slice(2 * blocks + 2 * tok, 3 * blocks + 2 * tok)

    def spectrum(b):
        parts = []
        for c in range(2):
            lanes = slice(c * tok, (c + 1) * tok)
            re, im = b[:blocks, lanes], b[blocks:, lanes]
            parts.append(jnp.concatenate([re * cos + im * sin, im * cos - re * sin], 1))
        return dot(jnp.concatenate(parts, 0).astype(BF16), table_ref[: 2 * tok, inner])

    wide[...] = got_ref[...].astype(F32)
    sig, causal, anti = [
        jnp.concatenate([wide[pl.ds(2 * a + c, blocks, stride=6), :] for c in range(2)], 1)
        for a in range(3)
    ]
    place = lax.broadcasted_iota(jnp.int32, (blocks, 2 * tok), 0)
    lane = lax.broadcasted_iota(jnp.int32, (blocks, 2 * tok), 1)
    anti = jnp.where((place == 0) & (lane % tok == 0), 0.0, anti)
    f = spectrum(dot(table_ref[:, : 2 * blocks], jnp.concatenate([causal, anti], 0).astype(BF16)))
    s = spectrum(dot(table_ref[:, :blocks], sig.astype(BF16)))

    sr, si, fr, fi = s[:, :tok], s[:, tok:], f[:, :tok], f[:, tok:]
    y = jnp.concatenate([sr * fr - si * fi, sr * fi + si * fr], 1)
    g = dot(y.astype(BF16), table_ref[2 * tok : 4 * tok, inner])
    real, imag = [], []
    for c in range(2):
        re, im = g[c * blocks : (c + 1) * blocks, :tok], g[c * blocks : (c + 1) * blocks, tok:]
        real.append(re * cos - im * sin)
        imag.append(re * sin + im * cos)
    out = dot(table_ref[:blocks, back], jnp.concatenate(real, 1).astype(BF16))
    out += dot(table_ref[blocks : 2 * blocks, back], jnp.concatenate(imag, 1).astype(BF16))
    for c in range(2):
        buf[pl.ds(c, blocks, stride=2), :] = out[:, c * tok : (c + 1) * tok]
    out_ref[...] = buf[...].astype(BF16)


def last_kernel(conv_ref, second_ref, direct_ref, w_ref, out_ref):
    gated = (second_ref[...] * (conv_ref[...].astype(F32) + direct_ref[...])).astype(BF16)
    out_ref[...] = lax.dot_general(
        gated, w_ref[...], (((0,), (0,)), ((), ())), preferred_element_type=F32
    ).astype(BF16)


def call(kernel, outs, scratch=(), **specs):
    return pl.pallas_call(
        kernel,
        out_shape=outs,
        scratch_shapes=list(scratch),
        compiler_params=pltpu.CompilerParams(vmem_limit_bytes=24 * 1024 * 1024),
        **specs,
    )


def exchange(x):
    return lax.all_to_all(x, AXES, split_axis=0, concat_axis=0, tiled=True)


def body(tokens, w_in, conv_taps, causal_taps, anticausal_taps, skip_gain, w_out):
    rows = tokens.shape[0]
    channels, width = w_out.shape
    count = lax.axis_size(AXES)
    shape = jax.ShapeDtypeStruct
    vmem = pltpu.VMEM
    table, twist = tables(count, rows)

    before = lax.ppermute(tokens[-8:], AXES, [(i, i + 1) for i in range(count - 1)])
    after = lax.ppermute(tokens[:8], AXES, [(i + 1, i) for i in range(count - 1)])
    in_vmem, hbm = pl.BlockSpec(memory_space=vmem), pl.BlockSpec(memory_space=pltpu.HBM)
    send, second, direct, table, twist = call(
        front_kernel,
        [
            shape((3 * channels, rows), BF16),
            shape((channels, rows), F32),
            shape((channels, rows), F32),
            shape(table.shape, table.dtype),
            shape(twist.shape, twist.dtype),
        ],
        [vmem((channels, rows), F32), vmem((3 * channels, rows), F32), pltpu.SemaphoreType.DMA((2,))],
        in_specs=[in_vmem] * 8 + [hbm] * 2,
        out_specs=[in_vmem] * 5,
    )(tokens, before, after, w_in, conv_taps, skip_gain[None], causal_taps, anticausal_taps, table, twist)
    got = exchange(send.reshape(-1, 2, rows)).reshape(send.shape)

    conv = call(
        conv_kernel,
        shape((channels, rows), BF16),
        [vmem((channels, rows), F32), vmem((3 * channels, rows), F32)],
    )(got, table, twist)
    conv = exchange(conv)
    return call(last_kernel, shape((rows, width), BF16))(conv, second, direct, w_out)


def solution(mesh):
    rows = P(AXES, None)
    in_specs = (rows, P(), P(), rows, rows, P(), P())
    return jax.shard_map(body, mesh=mesh, in_specs=in_specs, out_specs=rows, check_vma=False)
```

time: 94 us -> 76.1 us (0.81)
  starting transfers between devices: 24.5 us -> 7.06 us
  blocking collectives: 39.3 us -> 54.9 us
  waiting for transfers between devices: 12.4 us -> 1.14 us
  local copies, waits for them, and re-layouts: 11.6 us -> 8.98 us
  matrix products: 2.04 us -> 0 us
    all_to_all x1 -> x0, starting transfers between devices: 17.8 us -> none  [exchange(): return lax.all_to_all(x, AXES, split_axis=0, concat_axis=0, tiled=True)]
    all_to_all x2, blocking collectives: 39.3 us -> 54.9 us  [exchange(): return lax.all_to_all(x, AXES, split_axis=0, concat_axis=0, tiled=True)]
    all_to_all x1 -> x0, waiting for transfers between devices: 11 us -> none  [exchange(): return lax.all_to_all(x, AXES, split_axis=0, concat_axis=0, tiled=True)]
    unnamed x32 -> x18, local copies, waits for them, and re-layouts: 10.7 us -> 8.24 us
    dot_general x2 -> x0, matrix products: 2.04 us -> none  [dot(): return jnp.dot(a, b, preferred_element_type=F32)]
  transfers between devices with their start and end apart: 3 -> 2, of which waited for: 2 -> 1; matrix products, arithmetic and copies ran while one was open for 2% -> 0% of each run, Pallas kernels for 0% -> 0%
where the time goes in v1:
time: 76.1 us; the launch traced here: 75.6 us
  blocking collectives  54.9 us (72%)
  local copies, waits for them, and re-layouts  8.98 us (12%)
  starting transfers between devices  7.06 us (9%)
  Pallas kernels  3.45 us (5%)
  waiting for transfers between devices  1.14 us (1%)
    all_to_all x2, blocking collectives, exchange(): return lax.all_to_all(x, AXES, split_axis=0, concat_axis=0, tiled=True)  54.9 us
    unnamed x18, local copies, waits for them, and re-layouts  8.24 us
    ppermute x1, starting transfers between devices, body(): lax.ppermute(tokens[:8], AXES, [(i + 1, i) for i in range(count - 1)])  5.14 us
    ppermute x1, starting transfers between devices, body(): lax.ppermute(tokens[-8:], AXES, [(i, i + 1) for i in range(count - 1)])  1.92 us
  transfers between devices with their start and end apart: 2, of which 1 were waited for; matrix products, arithmetic and copies ran while one was open for 0% of the time, Pallas kernels for 0%

profile of v1, /device:TPU:1, one launch (start us, length us, event | category | flops | bytes accessed | tf_op | source)
XLA Modules:
  0.0 75.6 jit_solution(5394615411699958720)
XLA Ops:
  0.0 0.7 fusion
  0.7 5.1 %collective-permute-start.1 = (bf16[8,1024]{1,0:T(8,128)(2,1)S(1)}, bf16[8,1024]{1,0:T(8,128)(2,1)S(1)}, u32[]{:S(2)}, u32[]{:S(2)}) collective-permute-start(bf16[8,1024]{1,0:T(8,128)(2,1)S(1)} %get-tuple-element.15), channel_id=1, source_target_pairs={{1,0},{2,1},{3,2},{4,3},{5,4},{6,5},{7,6},{8,7},{9,8},{10,9},{11,1... | collective-permute-start | bytes 49160 | tf_op jit(solution)/shard_map/ppermute | solution.py:148
  5.9 1.9 %collective-permute-start = (bf16[8,1024]{1,0:T(8,128)(2,1)S(1)}, bf16[8,1024]{1,0:T(8,128)(2,1)S(1)}, u32[]{:S(2)}, u32[]{:S(2)}) collective-permute-start(bf16[8,1024]{1,0:T(8,128)(2,1)S(1)} %get-tuple-element.16), channel_id=1, source_target_pairs={{0,1},{1,2},{2,3},{3,4},{4,5},{5,6},{6,7},{7,8},{8,9},{9,10},{10,1... | collective-permute-start | bytes 49160 | tf_op jit(solution)/shard_map/ppermute | solution.py:147
  7.8 0.0 collective-permute-done.1.after_ref
  7.8 1.1 %collective-permute-done.before_ref = bf16[8,1024]{1,0:T(8,128)(2,1)S(1)} collective-permute-done((bf16[8,1024]{1,0:T(8,128)(2,1)S(1)}, bf16[8,1024]{1,0:T(8,128)(2,1)S(1)}, u32[]{:S(2)}, u32[]{:S(2)}) %collective-permute-start) | collective-permute-done | bytes 16416 | tf_op jit(solution)/shard_map/ppermute | solution.py:147
  9.0 0.0 copy-start
  9.0 1.9 %copy-done = bf16[1024,1536]{1,0:T(8,128)(2,1)S(1)} copy-done((bf16[1024,1536]{1,0:T(8,128)(2,1)S(1)}, bf16[1024,1536]{1,0:T(8,128)(2,1)}, u32[]{:S(2)}) %copy-start) | copy-done | bytes 3145752
  10.9 0.0 copy-start.2
  10.9 1.2 %copy-done.2 = bf16[512,1024]{1,0:T(8,128)(2,1)S(1)} copy-done((bf16[512,1024]{1,0:T(8,128)(2,1)S(1)}, bf16[512,1024]{1,0:T(8,128)(2,1)}, u32[]{:S(2)}) %copy-start.2) | copy-done | bytes 1048600
  12.1 0.0 copy-start.3
  12.1 0.9 %copy-done.3 = bf16[128,1024]{1,0:T(8,128)(2,1)S(1)} copy-done((bf16[128,1024]{1,0:T(8,128)(2,1)S(1)}, bf16[128,1024]{1,0:T(8,128)(2,1)}, u32[]{:S(2)}) %copy-start.3) | copy-done | bytes 262168
  13.0 0.0 copy-start.4
  13.0 0.9 %copy-done.4 = f32[256,256]{1,0:T(8,128)S(1)} copy-done((f32[256,256]{1,0:T(8,128)S(1)}, f32[256,256]{1,0:T(8,128)}, u32[]{:S(2)}) %copy-start.4) | copy-done | bytes 262168
  14.0 0.0 copy-start.5
  14.0 0.9 %copy-done.5 = bf16[128,512]{1,0:T(8,128)(2,1)S(1)} copy-done((bf16[128,512]{1,0:T(8,128)(2,1)S(1)}, bf16[128,512]{1,0:T(8,128)(2,1)}, u32[]{:S(2)}) %copy-start.5) | copy-done | bytes 131096
  14.9 0.0 copy-start.6
  14.9 0.9 %copy-done.6 = bf16[128,512]{1,0:T(8,128)(2,1)S(1)} copy-done((bf16[128,512]{1,0:T(8,128)(2,1)S(1)}, bf16[128,512]{1,0:T(8,128)(2,1)}, u32[]{:S(2)}) %copy-start.6) | copy-done | bytes 131096
  15.8 0.0 copy-start.7
  15.8 0.7 copy-done.7
  16.5 0.0 copy-start.8
  16.5 0.7 copy-done.8
  17.2 0.0 copy-start.1
  17.2 1.1 %shard_map.91 = (bf16[1536,128]{1,0:T(8,128)(2,1)S(1)}, f32[512,128]{1,0:T(8,128)S(1)}, f32[512,128]{1,0:T(8,128)S(1)}, bf16[512,1024]{1,0:T(8,128)(2,1)S(1)}, f32[256,256]{1,0:T(8,128)S(1)}) custom-call(bf16[128,1024]{1,0:T(8,128)(2,1)S(1)} %copy-done.3, bf16[8,1024]{1,0:T(8,128)(2,1)S(1)} %collective-permute-done.before_ref, ...), custom_call_target="tpu_custom_call" | custom-call | tf_op jit(solution)/shard_map/pallas_call | solution.py:150
  18.3 35.9 %all_to_all.16 = bf16[768,2,128]{2,1,0:T(2,128)(2,1)S(1)} all-to-all(bf16[768,2,128]{2,1,0:T(2,128)(2,1)S(1)} %bitcast.8), channel_id=1, replica_groups=mesh['blk'=8,'fft'=32] {'blk','fft'}, dimensions={0} | all-to-all | bytes 786432 | tf_op jit(solution)/shard_map/all_to_all | solution.py:136
  54.2 1.3 %shard_map.92 = bf16[512,128]{1,0:T(8,128)(2,1)S(1)} custom-call(bf16[1536,128]{1,0:T(8,128)(2,1)S(1)} %bitcast.5, bf16[512,1024]{1,0:T(8,128)(2,1)S(1)} %get-tuple-element.11.table_ref, f32[256,256]{1,0:T(8,128)S(1)} %get-tuple-element.12.twist_ref), custom_call_target="tpu_custom_call" | custom-call | tf_op jit(solution)/shard_map/pallas_call | solution.py:165
  55.5 19.0 %all_to_all.17 = bf16[256,2,128]{2,1,0:T(2,128)(2,1)S(1)} all-to-all(bf16[256,2,128]{2,1,0:T(2,128)(2,1)S(1)} %bitcast.6), channel_id=1, replica_groups=mesh['blk'=8,'fft'=32] {'blk','fft'}, dimensions={0} | all-to-all | bytes 262144 | tf_op jit(solution)/shard_map/all_to_all | solution.py:136
  74.5 0.0 copy-done.1
  74.5 1.0 %shard_map.93 = bf16[128,1024]{1,0:T(8,128)(2,1)} custom-call(bf16[512,128]{1,0:T(8,128)(2,1)S(1)} %bitcast.7, f32[512,128]{1,0:T(8,128)S(1)} %get-tuple-element.13.second_ref, f32[512,128]{1,0:T(8,128)S(1)} %get-tuple-element.14.direct_ref, bf16[512,1024]{1,0:T(8,128)(2,1)S(1)} %copy-done.1), custom_call_target="tpu_custom_call" | custom-call | tf_op jit(solution)/shard_map/pallas_call | solution.py:171
Async XLA Ops:
  0.7 7.1 %collective-permute-start.1 = (bf16[8,1024]{1,0:T(8,128)(2,1)S(1)}, bf16[8,1024]{1,0:T(8,128)(2,1)S(1)}, u32[]{:S(2)}, u32[]{:S(2)}) collective-permute-start(bf16[8,1024]{1,0:T(8,128)(2,1)S(1)} %get-tuple-element.15), channel_id=1, source_target_pairs={{1,0},{2,1},{3,2},{4,3},{5,4},{6,5},{7,6},{8,7},{9,8},{10,9},{11,1... | collective-permute-start | bytes 49160 | tf_op jit(solution)/shard_map/ppermute | solution.py:148
  5.9 3.1 %collective-permute-start = (bf16[8,1024]{1,0:T(8,128)(2,1)S(1)}, bf16[8,1024]{1,0:T(8,128)(2,1)S(1)}, u32[]{:S(2)}, u32[]{:S(2)}) collective-permute-start(bf16[8,1024]{1,0:T(8,128)(2,1)S(1)} %get-tuple-element.16), channel_id=1, source_target_pairs={{0,1},{1,2},{2,3},{3,4},{4,5},{5,6},{6,7},{7,8},{8,9},{9,10},{10,1... | collective-permute-start | bytes 49160 | tf_op jit(solution)/shard_map/ppermute | solution.py:147
  9.0 1.9 %copy-start = (bf16[1024,1536]{1,0:T(8,128)(2,1)S(1)}, bf16[1024,1536]{1,0:T(8,128)(2,1)}, u32[]{:S(2)}) copy-start(bf16[1024,1536]{1,0:T(8,128)(2,1)} %w_ref.2) | copy-start | bytes 9437188
  10.9 1.2 %copy-start.2 = (bf16[512,1024]{1,0:T(8,128)(2,1)S(1)}, bf16[512,1024]{1,0:T(8,128)(2,1)}, u32[]{:S(2)}) copy-start(bf16[512,1024]{1,0:T(8,128)(2,1)} %constant.4.clone.table_ref) | copy-start | bytes 3145732
  12.1 0.9 %copy-start.3 = (bf16[128,1024]{1,0:T(8,128)(2,1)S(1)}, bf16[128,1024]{1,0:T(8,128)(2,1)}, u32[]{:S(2)}) copy-start(bf16[128,1024]{1,0:T(8,128)(2,1)} %tok_ref.1) | copy-start | bytes 786436
  13.0 0.9 %copy-start.4 = (f32[256,256]{1,0:T(8,128)S(1)}, f32[256,256]{1,0:T(8,128)}, u32[]{:S(2)}) copy-start(f32[256,256]{1,0:T(8,128)} %constant.5.clone.twist_ref) | copy-start | bytes 786436
  14.0 0.9 %copy-start.5 = (bf16[128,512]{1,0:T(8,128)(2,1)S(1)}, bf16[128,512]{1,0:T(8,128)(2,1)}, u32[]{:S(2)}) copy-start(bf16[128,512]{1,0:T(8,128)(2,1)} %causal_ref.1) | copy-start | bytes 393220
  14.9 0.9 %copy-start.6 = (bf16[128,512]{1,0:T(8,128)(2,1)S(1)}, bf16[128,512]{1,0:T(8,128)(2,1)}, u32[]{:S(2)}) copy-start(bf16[128,512]{1,0:T(8,128)(2,1)} %anti_ref.1) | copy-start | bytes 393220
  15.8 0.7 copy-start.7
  16.5 0.7 copy-start.8
  17.2 57.3 %copy-start.1 = (bf16[512,1024]{1,0:T(8,128)(2,1)S(1)}, bf16[512,1024]{1,0:T(8,128)(2,1)}, u32[]{:S(2)}) copy-start(bf16[512,1024]{1,0:T(8,128)(2,1)} %w_ref.3) | copy-start | bytes 3145732

commit v2 on v1

v2 whole, which is shorter than its diff:
```python
import math

import jax
import jax.numpy as jnp
import numpy as np
from jax import lax
from jax.experimental import pallas as pl
from jax.experimental.pallas import tpu as pltpu
from jax.sharding import PartitionSpec as P

AXES = ("blk", "fft")
F32 = jnp.float32
BF16 = jnp.bfloat16


def tables(blocks, tok):
    length = 2 * blocks * tok
    half = np.arange(blocks) + 0.5
    ang = 2 * math.pi * np.outer(half, np.arange(2 * blocks)) / (2 * blocks)
    fore = np.concatenate([np.cos(ang), -np.sin(ang)], 0)
    back = np.concatenate([fore[:blocks, :blocks].T, fore[blocks:, :blocks].T], 0) * (2 / length)
    fore[:, blocks:] *= -1
    twist = 2 * math.pi * np.outer(half, np.arange(tok)) / length
    inner = 2 * math.pi * np.outer(np.arange(tok), np.arange(tok)) / tok
    c, s = np.cos(inner), np.sin(inner)
    inner = np.block([[c, -s], [s, c], [c, s], [-s, c]])
    return (
        jnp.asarray(np.concatenate([fore, inner, back], 1), BF16),
        jnp.asarray(np.concatenate([np.cos(twist), np.sin(twist)], 1), F32),
    )


def dot(a, b):
    return jnp.dot(a, b, preferred_element_type=F32)


def front_kernel(
    tok_hbm, w_hbm, taps_hbm, skip_hbm, causal_hbm, anti_hbm,
    send_ref, second_ref, direct_ref,
    tok_ref, w_ref, taps_ref, skip_ref, causal_ref, anti_ref, buf, wide, sems,
):
    rows = tok_ref.shape[0]
    channels = causal_ref.shape[1]
    half = channels // 2

    def slab(i):
        return slice(i * channels, (i + 1) * channels)

    pairs = [(causal_hbm, causal_ref), (anti_hbm, anti_ref), (tok_hbm, tok_ref)]
    pairs += [(w_hbm.at[:, slab(i)], w_ref.at[:, slab(i)]) for i in (0, 2, 1)]
    pairs += [(taps_hbm, taps_ref), (skip_hbm, skip_ref)]
    copies = [pltpu.make_async_copy(a, b, sems.at[i]) for i, (a, b) in enumerate(pairs)]
    for copy in copies:
        copy.start()

    def place(a, block):
        buf[...] = block.T
        for c in range(2):
            wide[pl.ds(2 * a + c, half, stride=8), :] = buf[pl.ds(c, half, stride=2), :]

    copies[0].wait()
    place(1, causal_ref[...].astype(F32))
    copies[1].wait()
    place(2, anti_ref[...].astype(F32))
    copies[6].wait()
    copies[7].wait()
    copies[2].wait()
    row = lax.broadcasted_iota(jnp.int32, (rows, channels), 0)

    def short(i, copy):
        copy.wait()
        proj = dot(tok_ref[...], w_ref[:, slab(i)]).astype(BF16).astype(F32)
        prior, here, after = [taps_ref[k : k + 1, slab(i)] for k in range(3)]
        up = jnp.where(row == 0, 0.0, pltpu.roll(proj, 1, 0))
        down = jnp.where(row == rows - 1, 0.0, pltpu.roll(proj, rows - 1, 0))
        return prior * up + here * proj + after * down, after * proj[:1], prior * proj[rows - 1 :]

    first, first_up, first_down = short(0, copies[3])
    value, value_up, value_down = short(2, copies[4])
    signal = first * value
    place(0, signal)
    direct_ref[...] = (skip_ref[...] * signal).T
    second, second_up, second_down = short(1, copies[5])
    second_ref[...] = second.T
    last = rows - 1
    ends = [
        first[:1], value[last:], value[:1], second[last:], second[:1],
        first_up, first_down, value_up, value_down, second_up, second_down,
        skip_ref[...], skip_ref[...],
    ]
    fill = jnp.zeros((rows - len(ends) - 1, channels), F32)
    place(3, jnp.concatenate(ends + [fill, first[last:]], 0))
    send_ref[...] = wide[...].astype(BF16)


def conv_kernel(got_ref, table_ref, twist_ref, out_ref, buf, wide):
    tok = got_ref.shape[1]
    blocks = got_ref.shape[0] // 8
    cos, sin = twist_ref[:, :tok], twist_ref[:, tok:]
    inner = slice(2 * blocks, 2 * blocks + 2 * tok)
    back = slice(2 * blocks + 2 * tok, 3 * blocks + 2 * tok)
    place = lax.broadcasted_iota(jnp.int32, (blocks, tok), 0)
    lane = lax.broadcasted_iota(jnp.int32, (blocks, tok), 1)
    at_end = (lane == 0) | (lane == tok - 1)

    def left(x, n):
        return pltpu.roll(x, tok - n, 1)

    def take(a, c):
        return wide[pl.ds(2 * a + c, blocks, stride=8), :]

    def spectrum(b):
        parts = []
        for c in range(2):
            lanes = slice(c * tok, (c + 1) * tok)
            re, im = b[:blocks, lanes], b[blocks:, lanes]
            parts.append(jnp.concatenate([re * cos + im * sin, im * cos - re * sin], 1))
        return dot(jnp.concatenate(parts, 0).astype(BF16), table_ref[: 2 * tok, inner])

    wide[...] = got_ref[...].astype(F32)
    causal = jnp.concatenate([take(1, 0), take(1, 1)], 1)
    anti = jnp.concatenate(
        [jnp.where((place == 0) & (lane == 0), 0.0, take(2, c)) for c in range(2)], 1
    )
    f = spectrum(dot(table_ref[:, : 2 * blocks], jnp.concatenate([causal, anti], 0).astype(BF16)))

    signal, end_signal, end_second, end_skip = [], [], [], []
    for c in range(2):
        ends = take(3, c)
        prior = jnp.where(place == 0, 0.0, pltpu.roll(ends, 1, 0))
        after = jnp.where(place == blocks - 1, 0.0, pltpu.roll(ends, blocks - 1, 0))
        full = ends + left(jnp.where(lane % 2 == 1, after, prior), 6)
        end_signal.append(full * left(full, 2))
        end_second.append(left(full, 4))
        end_skip.append(left(ends, 12))
        signal.append(jnp.where(at_end, end_signal[c], take(0, c)))
    s = spectrum(dot(table_ref[:, :blocks], jnp.concatenate(signal, 1).astype(BF16)))

    sr, si, fr, fi = s[:, :tok], s[:, tok:], f[:, :tok], f[:, tok:]
    y = jnp.concatenate([sr * fr - si * fi, sr * fi + si * fr], 1)
    g = dot(y.astype(BF16), table_ref[2 * tok : 4 * tok, inner])
    real, imag = [], []
    for c in range(2):
        re, im = g[c * blocks : (c + 1) * blocks, :tok], g[c * blocks : (c + 1) * blocks, tok:]
        real.append(re * cos - im * sin)
        imag.append(re * sin + im * cos)
    out = dot(table_ref[:blocks, back], jnp.concatenate(real, 1).astype(BF16))
    out += dot(table_ref[blocks : 2 * blocks, back], jnp.concatenate(imag, 1).astype(BF16))
    for c in range(2):
        conv = out[:, c * tok : (c + 1) * tok]
        gated = end_second[c] * (conv + end_skip[c] * end_signal[c])
        buf[pl.ds(c, blocks, stride=2), :] = jnp.where(at_end, gated, conv)
    out_ref[...] = buf[...].astype(BF16)


def last_kernel(conv_ref, second_ref, direct_ref, w_ref, out_ref):
    conv = conv_ref[...].astype(F32)
    lane = lax.broadcasted_iota(jnp.int32, conv.shape, 1)
    at_end = (lane == 0) | (lane == conv.shape[1] - 1)
    gated = jnp.where(at_end, conv, second_ref[...] * (conv + direct_ref[...])).astype(BF16)
    out_ref[...] = lax.dot_general(
        gated, w_ref[...], (((0,), (0,)), ((), ())), preferred_element_type=F32
    ).astype(BF16)


def call(kernel, outs, scratch=(), mib=24, **specs):
    return pl.pallas_call(
        kernel,
        out_shape=outs,
        scratch_shapes=list(scratch),
        compiler_params=pltpu.CompilerParams(vmem_limit_bytes=mib * 1024 * 1024),
        **specs,
    )


def exchange(x):
    return lax.all_to_all(x, AXES, split_axis=0, concat_axis=0, tiled=True)


def body(tokens, w_in, conv_taps, causal_taps, anticausal_taps, skip_gain, w_out):
    rows = tokens.shape[0]
    channels, width = w_out.shape
    count = lax.axis_size(AXES)
    shape = jax.ShapeDtypeStruct
    vmem = pltpu.VMEM
    table, twist = tables(count, rows)

    hbm = pl.BlockSpec(memory_space=pltpu.HBM)
    staged = (tokens, w_in, conv_taps, skip_gain[None], causal_taps, anticausal_taps)
    send, second, direct = call(
        front_kernel,
        [shape((4 * channels, rows), BF16), shape((channels, rows), F32), shape((channels, rows), F32)],
        [vmem(x.shape, x.dtype) for x in staged]
        + [vmem((channels, rows), F32), vmem((4 * channels, rows), F32), pltpu.SemaphoreType.DMA((8,))],
        mib=60,
        in_specs=[hbm] * 6,
    )(*staged)
    got = exchange(send.reshape(count, 8, rows)).reshape(send.shape)

    conv = call(
        conv_kernel,
        shape((channels, rows), BF16),
        [vmem((channels, rows), F32), vmem((4 * channels, rows), F32)],
    )(got, table, twist)
    conv = exchange(conv)
    return call(last_kernel, shape((rows, width), BF16))(conv, second, direct, w_out)


def solution(mesh):
    rows = P(AXES, None)
    in_specs = (rows, P(), P(), rows, rows, P(), P())
    return jax.shard_map(body, mesh=mesh, in_specs=in_specs, out_specs=rows, check_vma=False)
```

time: 76.1 us -> 61.8 us (0.81)
  local copies, waits for them, and re-layouts: 8.98 us -> 0.02 us
  starting transfers between devices: 7.06 us -> 0 us
  Pallas kernels: 3.45 us -> 7.03 us
  waiting for transfers between devices: 1.14 us -> 0 us
    unnamed x18 -> x10, local copies, waits for them, and re-layouts: 8.24 us -> 0.02 us
    ppermute x2 -> x0, starting transfers between devices: 7.06 us -> none  [the longest x1 5.14 us: body(): lax.ppermute(tokens[:8], AXES, [(i + 1, i) for i in range(count - 1)])]
    pallas_call x1, Pallas kernels: 1.08 us -> 4.54 us  [body(): call(front_kernel, [shape((4 * channels, rows), BF16), shape((channels, r...]
    ppermute x2 -> x0, waiting for transfers between devices: 1.14 us -> none  [the longest x1 1.14 us: body(): lax.ppermute(tokens[-8:], AXES, [(i, i + 1) for i in range(count - 1)])]
  transfers between devices with their start and end apart: 2 -> 0, of which waited for: 1 -> 0; matrix products, arithmetic and copies ran while one was open for 0% -> 0% of each run, Pallas kernels for 0% -> 0%
where the time goes in v2:
time: 61.8 us; the launch traced here: 61.7 us
  blocking collectives  54.6 us (88%)
  Pallas kernels  7.03 us (11%)
    all_to_all x2, blocking collectives, exchange(): return lax.all_to_all(x, AXES, split_axis=0, concat_axis=0, tiled=True)  54.6 us
    pallas_call x1, Pallas kernels, body(): call(front_kernel, [shape((4 * channels, rows), BF16), shape((channels, r...  4.54 us
    pallas_call x1, Pallas kernels, body(): call(conv_kernel, shape((channels, rows), BF16), [vmem((channels, rows),...  1.44 us

profile of v2, /device:TPU:1, one launch (start us, length us, event | category | flops | bytes accessed | tf_op | source)
XLA Modules:
  0.0 61.7 jit_solution(6258438347332009704)
XLA Ops:
  0.0 0.0 copy-start.2
  0.0 0.0 copy-start.1
  0.0 0.0 copy-start
  0.0 4.5 %shard_map.91 = (bf16[2048,128]{1,0:T(8,128)(2,1)}, f32[512,128]{1,0:T(8,128)}, f32[512,128]{1,0:T(8,128)}) custom-call(bf16[128,1024]{1,0:T(8,128)(2,1)} %tok_hbm.1, bf16[1024,1536]{1,0:T(8,128)(2,1)} %w_hbm.1, f32[3,1536]{1,0:T(4,128)} %taps_hbm.1, f32[1,512]{1,0:T(1,128)} %bitcast.9, bf16[128,512]{1,0:T(8,128)(2,1)} %causal_hbm.1, bf16[128,512]{1,0:T(8,128)(2,1)} %anti_hbm.1), custom_call_target="tpu_custom_call" | custom-call | tf_op jit(solution)/shard_map/pallas_call | solution.py:190
  4.6 0.0 copy-start.3
  4.6 0.0 copy-start.4
  4.6 35.6 %all_to_all.16 = bf16[256,8,128]{2,1,0:T(8,128)(2,1)S(1)} all-to-all(bf16[256,8,128]{2,1,0:T(8,128)(2,1)} %bitcast.8), channel_id=1, replica_groups=mesh['blk'=8,'fft'=32] {'blk','fft'}, dimensions={0} | all-to-all | bytes 1048576 | tf_op jit(solution)/shard_map/all_to_all | solution.py:177
  40.2 0.0 copy-done.2
  40.2 0.0 copy-done.1
  40.2 1.4 %shard_map.92 = bf16[512,128]{1,0:T(8,128)(2,1)S(1)} custom-call(bf16[2048,128]{1,0:T(8,128)(2,1)S(1)} %bitcast.5, bf16[512,1024]{1,0:T(8,128)(2,1)S(1)} %copy-done.1, f32[256,256]{1,0:T(8,128)S(1)} %copy-done.2), custom_call_target="tpu_custom_call" | custom-call | tf_op jit(solution)/shard_map/pallas_call | solution.py:200
  41.7 18.9 %all_to_all.17 = bf16[256,2,128]{2,1,0:T(2,128)(2,1)S(1)} all-to-all(bf16[256,2,128]{2,1,0:T(2,128)(2,1)S(1)} %bitcast.7), channel_id=1, replica_groups=mesh['blk'=8,'fft'=32] {'blk','fft'}, dimensions={0} | all-to-all | bytes 262144 | tf_op jit(solution)/shard_map/all_to_all | solution.py:177
  60.6 0.0 copy-done
  60.6 0.0 copy-done.3
  60.6 0.0 copy-done.4
  60.6 1.0 %shard_map.93 = bf16[128,1024]{1,0:T(8,128)(2,1)} custom-call(bf16[512,128]{1,0:T(8,128)(2,1)S(1)} %bitcast.6, f32[512,128]{1,0:T(8,128)S(1)} %copy-done.3, f32[512,128]{1,0:T(8,128)S(1)} %copy-done.4, bf16[512,1024]{1,0:T(8,128)(2,1)S(1)} %copy-done), custom_call_target="tpu_custom_call" | custom-call | tf_op jit(solution)/shard_map/pallas_call | solution.py:206
Async XLA Ops:
  0.0 40.2 %copy-start.2 = (f32[256,256]{1,0:T(8,128)S(1)}, f32[256,256]{1,0:T(8,128)}, u32[]{:S(2)}) copy-start(f32[256,256]{1,0:T(8,128)} %constant.5.clone.twist_ref) | copy-start | bytes 786436
  0.0 40.2 %copy-start.1 = (bf16[512,1024]{1,0:T(8,128)(2,1)S(1)}, bf16[512,1024]{1,0:T(8,128)(2,1)}, u32[]{:S(2)}) copy-start(bf16[512,1024]{1,0:T(8,128)(2,1)} %constant.4.clone.table_ref) | copy-start | bytes 3145732
  0.0 60.6 %copy-start = (bf16[512,1024]{1,0:T(8,128)(2,1)S(1)}, bf16[512,1024]{1,0:T(8,128)(2,1)}, u32[]{:S(2)}) copy-start(bf16[512,1024]{1,0:T(8,128)(2,1)} %w_ref.1) | copy-start | bytes 3145732
  4.6 56.0 %copy-start.3 = (f32[512,128]{1,0:T(8,128)S(1)}, f32[512,128]{1,0:T(8,128)}, u32[]{:S(2)}) copy-start(f32[512,128]{1,0:T(8,128)} %get-tuple-element.9.second_ref) | copy-start | bytes 786436
  4.6 56.0 %copy-start.4 = (f32[512,128]{1,0:T(8,128)S(1)}, f32[512,128]{1,0:T(8,128)}, u32[]{:S(2)}) copy-start(f32[512,128]{1,0:T(8,128)} %get-tuple-element.10.direct_ref) | copy-start | bytes 786436

commit v3 on v2

--- a/solution.py
+++ b/solution.py
@@ -34,53 +34,42 @@
     return jnp.dot(a, b, preferred_element_type=F32)
 
 
+def first_kernel(out_ref):
+    out_ref[...] = jnp.zeros_like(out_ref)
+
+
 def front_kernel(
-    tok_hbm, w_hbm, taps_hbm, skip_hbm, causal_hbm, anti_hbm,
-    send_ref, second_ref, direct_ref,
-    tok_ref, w_ref, taps_ref, skip_ref, causal_ref, anti_ref, buf, wide, sems,
+    start_ref, tok_ref, w_ref, taps_ref, skip_ref, causal_ref, anti_ref,
+    send_ref, second_ref, direct_ref, buf, wide,
 ):
     rows = tok_ref.shape[0]
     channels = causal_ref.shape[1]
     half = channels // 2
+    row = lax.broadcasted_iota(jnp.int32, (rows, channels), 0)
 
     def slab(i):
         return slice(i * channels, (i + 1) * channels)
-
-    pairs = [(causal_hbm, causal_ref), (anti_hbm, anti_ref), (tok_hbm, tok_ref)]
-    pairs += [(w_hbm.at[:, slab(i)], w_ref.at[:, slab(i)]) for i in (0, 2, 1)]
-    pairs += [(taps_hbm, taps_ref), (skip_hbm, skip_ref)]
-    copies = [pltpu.make_async_copy(a, b, sems.at[i]) for i, (a, b) in enumerate(pairs)]
-    for copy in copies:
-        copy.start()
 
     def place(a, block):
         buf[...] = block.T
         for c in range(2):
             wide[pl.ds(2 * a + c, half, stride=8), :] = buf[pl.ds(c, half, stride=2), :]
 
-    copies[0].wait()
-    place(1, causal_ref[...].astype(F32))
-    copies[1].wait()
-    place(2, anti_ref[...].astype(F32))
-    copies[6].wait()
-    copies[7].wait()
-    copies[2].wait()
-    row = lax.broadcasted_iota(jnp.int32, (rows, channels), 0)
-
-    def short(i, copy):
-        copy.wait()
+    def short(i):
         proj = dot(tok_ref[...], w_ref[:, slab(i)]).astype(BF16).astype(F32)
         prior, here, after = [taps_ref[k : k + 1, slab(i)] for k in range(3)]
         up = jnp.where(row == 0, 0.0, pltpu.roll(proj, 1, 0))
         down = jnp.where(row == rows - 1, 0.0, pltpu.roll(proj, rows - 1, 0))
         return prior * up + here * proj + after * down, after * proj[:1], prior * proj[rows - 1 :]
 
-    first, first_up, first_down = short(0, copies[3])
-    value, value_up, value_down = short(2, copies[4])
+    place(1, causal_ref[...].astype(F32))
+    place(2, anti_ref[...].astype(F32))
+    first, first_up, first_down = short(0)
+    value, value_up, value_down = short(2)
     signal = first * value
     place(0, signal)
     direct_ref[...] = (skip_ref[...] * signal).T
-    second, second_up, second_down = short(1, copies[5])
+    second, second_up, second_down = short(1)
     second_ref[...] = second.T
     last = rows - 1
     ends = [
@@ -163,12 +152,13 @@
     ).astype(BF16)
 
 
-def call(kernel, outs, scratch=(), mib=24, **specs):
+def call(kernel, outs, scratch=(), mib=24, cost=0, **specs):
     return pl.pallas_call(
         kernel,
         out_shape=outs,
         scratch_shapes=list(scratch),
         compiler_params=pltpu.CompilerParams(vmem_limit_bytes=mib * 1024 * 1024),
+        cost_estimate=pl.CostEstimate(flops=cost, bytes_accessed=0, transcendentals=0) if cost else None,
         **specs,
     )
 
@@ -185,16 +175,13 @@
     vmem = pltpu.VMEM
     table, twist = tables(count, rows)
 
-    hbm = pl.BlockSpec(memory_space=pltpu.HBM)
     staged = (tokens, w_in, conv_taps, skip_gain[None], causal_taps, anticausal_taps)
+    start = call(first_kernel, shape((8, 128), F32), cost=20000000000)()
     send, second, direct = call(
         front_kernel,
         [shape((4 * channels, rows), BF16), shape((channels, rows), F32), shape((channels, rows), F32)],
-        [vmem(x.shape, x.dtype) for x in staged]
-        + [vmem((channels, rows), F32), vmem((4 * channels, rows), F32), pltpu.SemaphoreType.DMA((8,))],
-        mib=60,
-        in_specs=[hbm] * 6,
-    )(*staged)
+        [vmem((channels, rows), F32), vmem((4 * channels, rows), F32)],
+    )(start, *staged)
     got = exchange(send.reshape(count, 8, rows)).reshape(send.shape)
 
     conv = call(

time: 61.8 us -> 60.2 us (0.974)
  Pallas kernels: 7.03 us -> 3.57 us
  local copies, waits for them, and re-layouts: 0.02 us -> 2.03 us
    pallas_call x1, Pallas kernels: 4.54 us -> 1.08 us  [body(): call(front_kernel, [shape((4 * channels, rows), BF16), shape((channels, r...]
    unnamed x10 -> x18, local copies, waits for them, and re-layouts: 0.02 us -> 2.03 us
where the time goes in v3:
time: 60.2 us; the launch traced here: 60 us
  blocking collectives  54.4 us (90%)
  Pallas kernels  3.57 us (6%)
  local copies, waits for them, and re-layouts  2.03 us (3%)
    all_to_all x2, blocking collectives, exchange(): return lax.all_to_all(x, AXES, split_axis=0, concat_axis=0, tiled=True)  54.4 us
    unnamed x18, local copies, waits for them, and re-layouts  2.03 us
    pallas_call x1, Pallas kernels, body(): call(conv_kernel, shape((channels, rows), BF16), [vmem((channels, rows),...  1.44 us

profile of v3, /device:TPU:1, one launch (start us, length us, event | category | flops | bytes accessed | tf_op | source)
XLA Modules:
  0.0 60.0 jit_solution(11472186367104899482)
XLA Ops:
  0.0 0.0 copy-start.8
  0.0 0.0 copy-start.6
  0.0 0.0 copy-start.5
  0.0 0.0 copy-start.7
  0.0 0.0 copy-start
  0.0 0.0 copy-start.3
  0.0 0.0 copy-start.2
  0.1 0.0 copy-start.4
  0.1 0.6 %copy-done.8 = f32[512]{0:T(512)S(1)} copy-done((f32[512]{0:T(512)S(1)}, f32[512]{0:T(512)}, u32[]{:S(2)}) %copy-start.8) | copy-done | bytes 2072
  0.7 0.2 copy-done.6
  0.9 0.1 copy-done.5
  1.0 0.0 copy-done.7
  1.0 1.1 %copy-done = bf16[1024,1536]{1,0:T(8,128)(2,1)S(1)} copy-done((bf16[1024,1536]{1,0:T(8,128)(2,1)S(1)}, bf16[1024,1536]{1,0:T(8,128)(2,1)}, u32[]{:S(2)}) %copy-start) | copy-done | bytes 3145752
  2.1 0.0 copy-done.3
  2.1 0.0 copy-start.1
  2.1 1.1 %shard_map.92 = (bf16[2048,128]{1,0:T(8,128)(2,1)S(1)}, f32[512,128]{1,0:T(8,128)S(1)}, f32[512,128]{1,0:T(8,128)S(1)}) custom-call(f32[8,128]{1,0:T(8,128)S(1)} %shard_map.91.start_ref, bf16[128,1024]{1,0:T(8,128)(2,1)S(1)} %copy-done.3, bf16[1024,1536]{1,0:T(8,128)(2,1)S(1)} %copy-done, f32[3,1536]{1,0:T(4,128)S(1)} %copy-done.7, f32[1,512]{1,0:T(1,128)S(1)} %bitcast.9, ...), custom_call_target="tpu_custom_call" | custom-call | tf_op jit(solution)/shard_map/pallas_call | solution.py:180
  3.2 35.4 %all_to_all.16 = bf16[256,8,128]{2,1,0:T(8,128)(2,1)S(1)} all-to-all(bf16[256,8,128]{2,1,0:T(8,128)(2,1)S(1)} %bitcast.6), channel_id=1, replica_groups=mesh['blk'=8,'fft'=32] {'blk','fft'}, dimensions={0} | all-to-all | bytes 1048576 | tf_op jit(solution)/shard_map/all_to_all | solution.py:167
  38.6 0.0 copy-done.2
  38.6 0.0 copy-done.4
  38.6 1.4 %shard_map.93 = bf16[512,128]{1,0:T(8,128)(2,1)S(1)} custom-call(bf16[2048,128]{1,0:T(8,128)(2,1)S(1)} %bitcast.5, bf16[512,1024]{1,0:T(8,128)(2,1)S(1)} %copy-done.2, f32[256,256]{1,0:T(8,128)S(1)} %copy-done.4), custom_call_target="tpu_custom_call" | custom-call | tf_op jit(solution)/shard_map/pallas_call | solution.py:187
  40.1 18.9 %all_to_all.17 = bf16[256,2,128]{2,1,0:T(2,128)(2,1)S(1)} all-to-all(bf16[256,2,128]{2,1,0:T(2,128)(2,1)S(1)} %bitcast.8), channel_id=1, replica_groups=mesh['blk'=8,'fft'=32] {'blk','fft'}, dimensions={0} | all-to-all | bytes 262144 | tf_op jit(solution)/shard_map/all_to_all | solution.py:167
  59.0 0.0 copy-done.1
  59.0 1.0 %shard_map.94 = bf16[128,1024]{1,0:T(8,128)(2,1)} custom-call(bf16[512,128]{1,0:T(8,128)(2,1)S(1)} %bitcast.7, f32[512,128]{1,0:T(8,128)S(1)} %get-tuple-element.9.second_ref, f32[512,128]{1,0:T(8,128)S(1)} %get-tuple-element.10.direct_ref, bf16[512,1024]{1,0:T(8,128)(2,1)S(1)} %copy-done.1), custom_call_target="tpu_custom_call" | custom-call | tf_op jit(solution)/shard_map/pallas_call | solution.py:193
  (1 shorter events, 0.0 us)
Async XLA Ops:
  0.0 0.7 %copy-start.8 = (f32[512]{0:T(512)S(1)}, f32[512]{0:T(512)}, u32[]{:S(2)}) copy-start(f32[512]{0:T(512)} %param.14) | copy-start | bytes 6148
  0.0 0.9 %copy-start.6 = (bf16[128,512]{1,0:T(8,128)(2,1)S(1)}, bf16[128,512]{1,0:T(8,128)(2,1)}, u32[]{:S(2)}) copy-start(bf16[128,512]{1,0:T(8,128)(2,1)} %anti_ref.1) | copy-start | bytes 393220
  0.0 1.0 %copy-start.5 = (bf16[128,512]{1,0:T(8,128)(2,1)S(1)}, bf16[128,512]{1,0:T(8,128)(2,1)}, u32[]{:S(2)}) copy-start(bf16[128,512]{1,0:T(8,128)(2,1)} %causal_ref.1) | copy-start | bytes 393220
  0.0 1.0 %copy-start.7 = (f32[3,1536]{1,0:T(4,128)S(1)}, f32[3,1536]{1,0:T(4,128)}, u32[]{:S(2)}) copy-start(f32[3,1536]{1,0:T(4,128)} %taps_ref.1) | copy-start | bytes 55300
  0.0 2.1 %copy-start = (bf16[1024,1536]{1,0:T(8,128)(2,1)S(1)}, bf16[1024,1536]{1,0:T(8,128)(2,1)}, u32[]{:S(2)}) copy-start(bf16[1024,1536]{1,0:T(8,128)(2,1)} %w_ref.2) | copy-start | bytes 9437188
  0.0 2.0 %copy-start.3 = (bf16[128,1024]{1,0:T(8,128)(2,1)S(1)}, bf16[128,1024]{1,0:T(8,128)(2,1)}, u32[]{:S(2)}) copy-start(bf16[128,1024]{1,0:T(8,128)(2,1)} %tok_ref.1) | copy-start | bytes 786436
  0.0 38.6 %copy-start.2 = (bf16[512,1024]{1,0:T(8,128)(2,1)S(1)}, bf16[512,1024]{1,0:T(8,128)(2,1)}, u32[]{:S(2)}) copy-start(bf16[512,1024]{1,0:T(8,128)(2,1)} %constant.4.clone.table_ref) | copy-start | bytes 3145732
  0.1 38.5 %copy-start.4 = (f32[256,256]{1,0:T(8,128)S(1)}, f32[256,256]{1,0:T(8,128)}, u32[]{:S(2)}) copy-start(f32[256,256]{1,0:T(8,128)} %constant.5.clone.twist_ref) | copy-start | bytes 786436
  2.1 56.9 %copy-start.1 = (bf16[512,1024]{1,0:T(8,128)(2,1)S(1)}, bf16[512,1024]{1,0:T(8,128)(2,1)}, u32[]{:S(2)}) copy-start(bf16[512,1024]{1,0:T(8,128)(2,1)} %w_ref.3) | copy-start | bytes 3145732

commit v4 on v3

--- a/solution.py
+++ b/solution.py
@@ -20,26 +20,27 @@
     fore = np.concatenate([np.cos(ang), -np.sin(ang)], 0)
     back = np.concatenate([fore[:blocks, :blocks].T, fore[blocks:, :blocks].T], 0) * (2 / length)
     fore[:, blocks:] *= -1
-    twist = 2 * math.pi * np.outer(half, np.arange(tok)) / length
     inner = 2 * math.pi * np.outer(np.arange(tok), np.arange(tok)) / tok
     c, s = np.cos(inner), np.sin(inner)
     inner = np.block([[c, -s], [s, c], [c, s], [-s, c]])
-    return (
-        jnp.asarray(np.concatenate([fore, inner, back], 1), BF16),
-        jnp.asarray(np.concatenate([np.cos(twist), np.sin(twist)], 1), F32),
-    )
+    return jnp.asarray(np.concatenate([fore, inner, back], 1), BF16)
 
 
 def dot(a, b):
     return jnp.dot(a, b, preferred_element_type=F32)
 
 
-def first_kernel(out_ref):
-    out_ref[...] = jnp.zeros_like(out_ref)
+def first_kernel(twist_ref):
+    blocks, tok = twist_ref.shape[0], twist_ref.shape[1] // 2
+    k = lax.broadcasted_iota(jnp.int32, (blocks, tok), 0)
+    t = lax.broadcasted_iota(jnp.int32, (blocks, tok), 1)
+    angle = ((2 * k + 1) * t).astype(F32) * (math.pi / (2 * blocks * tok))
+    twist_ref[:, :tok] = jnp.cos(angle)
+    twist_ref[:, tok:] = jnp.sin(angle)
 
 
 def front_kernel(
-    start_ref, tok_ref, w_ref, taps_ref, skip_ref, causal_ref, anti_ref,
+    _, tok_ref, w_ref, taps_ref, skip_ref, causal_ref, anti_ref,
     send_ref, second_ref, direct_ref, buf, wide,
 ):
     rows = tok_ref.shape[0]
@@ -104,7 +105,7 @@
             lanes = slice(c * tok, (c + 1) * tok)
             re, im = b[:blocks, lanes], b[blocks:, lanes]
             parts.append(jnp.concatenate([re * cos + im * sin, im * cos - re * sin], 1))
-        return dot(jnp.concatenate(parts, 0).astype(BF16), table_ref[: 2 * tok, inner])
+        return [dot(part.astype(BF16), table_ref[: 2 * tok, inner]) for part in parts]
 
     wide[...] = got_ref[...].astype(F32)
     causal = jnp.concatenate([take(1, 0), take(1, 1)], 1)
@@ -125,16 +126,16 @@
         signal.append(jnp.where(at_end, end_signal[c], take(0, c)))
     s = spectrum(dot(table_ref[:, :blocks], jnp.concatenate(signal, 1).astype(BF16)))
 
-    sr, si, fr, fi = s[:, :tok], s[:, tok:], f[:, :tok], f[:, tok:]
-    y = jnp.concatenate([sr * fr - si * fi, sr * fi + si * fr], 1)
-    g = dot(y.astype(BF16), table_ref[2 * tok : 4 * tok, inner])
     real, imag = [], []
     for c in range(2):
-        re, im = g[c * blocks : (c + 1) * blocks, :tok], g[c * blocks : (c + 1) * blocks, tok:]
+        sr, si, fr, fi = s[c][:, :tok], s[c][:, tok:], f[c][:, :tok], f[c][:, tok:]
+        y = jnp.concatenate([sr * fr - si * fi, sr * fi + si * fr], 1)
+        g = dot(y.astype(BF16), table_ref[2 * tok : 4 * tok, inner])
+        re, im = g[:, :tok], g[:, tok:]
         real.append(re * cos - im * sin)
         imag.append(re * sin + im * cos)
-    out = dot(table_ref[:blocks, back], jnp.concatenate(real, 1).astype(BF16))
-    out += dot(table_ref[blocks : 2 * blocks, back], jnp.concatenate(imag, 1).astype(BF16))
+    e = jnp.concatenate([jnp.concatenate(real, 1), jnp.concatenate(imag, 1)], 0)
+    out = dot(jnp.concatenate([table_ref[:blocks, back], table_ref[blocks : 2 * blocks, back]], 1), e.astype(BF16))
     for c in range(2):
         conv = out[:, c * tok : (c + 1) * tok]
         gated = end_second[c] * (conv + end_skip[c] * end_signal[c])
@@ -173,15 +174,15 @@
     count = lax.axis_size(AXES)
     shape = jax.ShapeDtypeStruct
     vmem = pltpu.VMEM
-    table, twist = tables(count, rows)
+    table = tables(count, rows)
 
     staged = (tokens, w_in, conv_taps, skip_gain[None], causal_taps, anticausal_taps)
-    start = call(first_kernel, shape((8, 128), F32), cost=20000000000)()
+    twist = call(first_kernel, shape((count, 2 * rows), F32), cost=2 * 10**9)()
     send, second, direct = call(
         front_kernel,
         [shape((4 * channels, rows), BF16), shape((channels, rows), F32), shape((channels, rows), F32)],
         [vmem((channels, rows), F32), vmem((4 * channels, rows), F32)],
-    )(start, *staged)
+    )(twist, *staged)
     got = exchange(send.reshape(count, 8, rows)).reshape(send.shape)
 
     conv = call(

time: 60.2 us -> 60.1 us (level)
    unnamed x18 -> x16, local copies, waits for them, and re-layouts: 2.03 us -> 1.54 us
where the time goes in v4:
time: 60.1 us; the launch traced here: 60 us
  blocking collectives  54.4 us (91%)
  Pallas kernels  3.99 us (7%)
  local copies, waits for them, and re-layouts  1.54 us (3%)
    all_to_all x2, blocking collectives, exchange(): return lax.all_to_all(x, AXES, split_axis=0, concat_axis=0, tiled=True)  54.4 us
    unnamed x16, local copies, waits for them, and re-layouts  1.54 us
    pallas_call x1, Pallas kernels, body(): call(conv_kernel, shape((channels, rows), BF16), [vmem((channels, rows),...  1.39 us

profile of v4, /device:TPU:1, one launch (start us, length us, event | category | flops | bytes accessed | tf_op | source)
XLA Modules:
  0.0 60.0 jit_solution(4787818080362398522)
XLA Ops:
  0.0 0.0 copy-start.7
  0.0 0.0 copy-start.5
  0.0 0.0 copy-start.4
  0.0 0.0 copy-start.6
  0.0 0.0 copy-start
  0.0 0.0 copy-start.3
  0.0 0.5 shard_map.82._.twist_ref
  0.5 0.0 copy-start.2
  0.6 0.1 copy-done.7
  0.7 0.2 copy-done.5
  0.9 0.1 copy-done.4
  1.0 0.0 copy-done.6
  1.0 1.1 %copy-done = bf16[1024,1536]{1,0:T(8,128)(2,1)S(1)} copy-done((bf16[1024,1536]{1,0:T(8,128)(2,1)S(1)}, bf16[1024,1536]{1,0:T(8,128)(2,1)}, u32[]{:S(2)}) %copy-start) | copy-done | bytes 3145752
  2.1 0.0 copy-done.3
  2.1 0.0 copy-start.1
  2.1 1.1 %shard_map.83 = (bf16[2048,128]{1,0:T(8,128)(2,1)S(1)}, f32[512,128]{1,0:T(8,128)S(1)}, f32[512,128]{1,0:T(8,128)S(1)}) custom-call(f32[256,256]{1,0:T(8,128)S(1)} %shard_map.82._.twist_ref, bf16[128,1024]{1,0:T(8,128)(2,1)S(1)} %copy-done.3, bf16[1024,1536]{1,0:T(8,128)(2,1)S(1)} %copy-done, f32[3,1536]{1,0:T(4,128)S(1)} %copy-done.6, ...), custom_call_target="tpu_custom_call" | custom-call | tf_op jit(solution)/shard_map/pallas_call | solution.py:181
  3.1 35.4 %all_to_all.16 = bf16[256,8,128]{2,1,0:T(8,128)(2,1)S(1)} all-to-all(bf16[256,8,128]{2,1,0:T(8,128)(2,1)S(1)} %bitcast.6), channel_id=1, replica_groups=mesh['blk'=8,'fft'=32] {'blk','fft'}, dimensions={0} | all-to-all | bytes 1048576 | tf_op jit(solution)/shard_map/all_to_all | solution.py:168
  38.6 0.0 copy-done.2
  38.6 1.4 %shard_map.84 = bf16[512,128]{1,0:T(8,128)(2,1)S(1)} custom-call(bf16[2048,128]{1,0:T(8,128)(2,1)S(1)} %bitcast.5, bf16[512,1024]{1,0:T(8,128)(2,1)S(1)} %copy-done.2, f32[256,256]{1,0:T(8,128)S(1)} %shard_map.82._.twist_ref), custom_call_target="tpu_custom_call" | custom-call | tf_op jit(solution)/shard_map/pallas_call | solution.py:188
  40.0 18.9 %all_to_all.17 = bf16[256,2,128]{2,1,0:T(2,128)(2,1)S(1)} all-to-all(bf16[256,2,128]{2,1,0:T(2,128)(2,1)S(1)} %bitcast.8), channel_id=1, replica_groups=mesh['blk'=8,'fft'=32] {'blk','fft'}, dimensions={0} | all-to-all | bytes 262144 | tf_op jit(solution)/shard_map/all_to_all | solution.py:168
  58.9 0.0 copy-done.1
  58.9 1.1 %shard_map.85 = bf16[128,1024]{1,0:T(8,128)(2,1)} custom-call(bf16[512,128]{1,0:T(8,128)(2,1)S(1)} %bitcast.7, f32[512,128]{1,0:T(8,128)S(1)} %get-tuple-element.9.second_ref, f32[512,128]{1,0:T(8,128)S(1)} %get-tuple-element.10.direct_ref, bf16[512,1024]{1,0:T(8,128)(2,1)S(1)} %copy-done.1), custom_call_target="tpu_custom_call" | custom-call | tf_op jit(solution)/shard_map/pallas_call | solution.py:194
Async XLA Ops:
  0.0 0.7 %copy-start.7 = (f32[512]{0:T(512)S(1)}, f32[512]{0:T(512)}, u32[]{:S(2)}) copy-start(f32[512]{0:T(512)} %param.13) | copy-start | bytes 6148
  0.0 0.9 %copy-start.5 = (bf16[128,512]{1,0:T(8,128)(2,1)S(1)}, bf16[128,512]{1,0:T(8,128)(2,1)}, u32[]{:S(2)}) copy-start(bf16[128,512]{1,0:T(8,128)(2,1)} %anti_ref.1) | copy-start | bytes 393220
  0.0 1.0 %copy-start.4 = (bf16[128,512]{1,0:T(8,128)(2,1)S(1)}, bf16[128,512]{1,0:T(8,128)(2,1)}, u32[]{:S(2)}) copy-start(bf16[128,512]{1,0:T(8,128)(2,1)} %causal_ref.1) | copy-start | bytes 393220
  0.0 1.0 %copy-start.6 = (f32[3,1536]{1,0:T(4,128)S(1)}, f32[3,1536]{1,0:T(4,128)}, u32[]{:S(2)}) copy-start(f32[3,1536]{1,0:T(4,128)} %taps_ref.1) | copy-start | bytes 55300
  0.0 2.1 %copy-start = (bf16[1024,1536]{1,0:T(8,128)(2,1)S(1)}, bf16[1024,1536]{1,0:T(8,128)(2,1)}, u32[]{:S(2)}) copy-start(bf16[1024,1536]{1,0:T(8,128)(2,1)} %w_ref.2) | copy-start | bytes 9437188
  0.0 2.0 %copy-start.3 = (bf16[128,1024]{1,0:T(8,128)(2,1)S(1)}, bf16[128,1024]{1,0:T(8,128)(2,1)}, u32[]{:S(2)}) copy-start(bf16[128,1024]{1,0:T(8,128)(2,1)} %tok_ref.1) | copy-start | bytes 786436
  0.5 38.0 %copy-start.2 = (bf16[512,1024]{1,0:T(8,128)(2,1)S(1)}, bf16[512,1024]{1,0:T(8,128)(2,1)}, u32[]{:S(2)}) copy-start(bf16[512,1024]{1,0:T(8,128)(2,1)} %constant.2.clone.table_ref) | copy-start | bytes 3145732
  2.1 56.8 %copy-start.1 = (bf16[512,1024]{1,0:T(8,128)(2,1)S(1)}, bf16[512,1024]{1,0:T(8,128)(2,1)}, u32[]{:S(2)}) copy-start(bf16[512,1024]{1,0:T(8,128)(2,1)} %w_ref.3) | copy-start | bytes 3145732

commit v5 on v4

v5 whole, which is shorter than its diff:
```python
import math

import jax
import jax.numpy as jnp
import numpy as np
from jax import lax
from jax.experimental import pallas as pl
from jax.experimental.pallas import tpu as pltpu
from jax.sharding import PartitionSpec as P

AXES = ("blk", "fft")
F32 = jnp.float32
BF16 = jnp.bfloat16


def tables(blocks, tok):
    length = 2 * blocks * tok
    half = np.arange(blocks) + 0.5
    ang = 2 * math.pi * np.outer(half, np.arange(2 * blocks)) / (2 * blocks)
    fore = np.concatenate([np.cos(ang), -np.sin(ang)], 0)
    back = np.concatenate([fore[:blocks, :blocks].T, fore[blocks:, :blocks].T], 0) * (2 / length)
    fore[:, blocks:] *= -1
    order = np.arange(blocks).reshape(-1, 2).T.reshape(-1)
    fore = fore[:, np.concatenate([order, order + blocks])]
    back = np.concatenate([back[:blocks][order], back[blocks:][order]], 0)
    inner = 2 * math.pi * np.outer(np.arange(tok), np.arange(tok)) / tok
    c, s = np.cos(inner), np.sin(inner)
    inner = np.block([[c, -s], [s, c], [c, s], [-s, c]])
    return jnp.asarray(np.concatenate([fore, inner, back], 1), BF16)


def dot(a, b):
    return jnp.dot(a, b, preferred_element_type=F32)


def first_kernel(twist_ref):
    blocks, tok = twist_ref.shape[0], twist_ref.shape[1] // 2
    k = lax.broadcasted_iota(jnp.int32, (blocks, tok), 0)
    t = lax.broadcasted_iota(jnp.int32, (blocks, tok), 1)
    angle = ((2 * k + 1) * t).astype(F32) * (math.pi / (2 * blocks * tok))
    twist_ref[:, :tok] = jnp.cos(angle)
    twist_ref[:, tok:] = jnp.sin(angle)


def front_kernel(
    _, tok_ref, tok_mate_ref, w_ref, taps_ref, causal_ref, causal_mate_ref, anti_ref, anti_mate_ref,
    send_ref, second_ref, tok, ends_ref, buf, wide,
):
    rows = tok_ref.shape[0]
    channels = causal_ref.shape[1]
    half = channels // 2
    chips = wide.shape[0] // 14
    core = lax.axis_index("fft") % 2
    last = 2 * rows - 1

    def mine(i):
        return pl.ds(pl.multiple_of(i * channels + core * half, half), half)

    def place(at, block):
        buf[...] = block.T
        for c in range(2):
            wide[pl.ds(at + c, chips, stride=14), :] = buf[pl.ds(c, chips, stride=2), :]

    own_rows = pl.ds(pl.multiple_of(core * rows, rows), rows)
    tok[own_rows, :] = tok_ref[...]
    tok[pl.ds(pl.multiple_of((1 - core) * rows, rows), rows), :] = tok_mate_ref[...]

    for a, (ref, mate_ref) in enumerate(((causal_ref, causal_mate_ref), (anti_ref, anti_mate_ref))):
        own, mate = ref[:, mine(0)].astype(F32), mate_ref[:, mine(0)].astype(F32)
        place(4 * a + 4, jnp.where(core == 0, own, mate))
        place(4 * a + 6, jnp.where(core == 0, mate, own))

    def short(i, cols):
        proj = dot(tok[...], w_ref[:, cols]).astype(BF16).astype(F32)
        row = lax.broadcasted_iota(jnp.int32, proj.shape, 0)
        prior, here, after = [taps_ref[k : k + 1, cols] for k in range(3)]
        up = jnp.where(row == 0, 0.0, pltpu.roll(proj, 1, 0))
        down = jnp.where(row == last, 0.0, pltpu.roll(proj, last, 0))
        return prior * up + here * proj + after * down, after * proj[:1], prior * proj[last:]

    first, first_up, first_down = short(0, mine(0))
    value, value_up, value_down = short(2, mine(2))
    signal = first * value
    place(0, signal[:rows])
    place(2, signal[rows:])
    cols = slice(channels, 2 * channels)
    near = jnp.concatenate([tok_ref[...], tok_mate_ref[:8], tok_mate_ref[rows - 8 :]], 0)
    proj = dot(near, w_ref[:, cols]).astype(BF16).astype(F32)
    own, mate = proj[:rows], proj[rows:]
    row = lax.broadcasted_iota(jnp.int32, own.shape, 0)
    prior, here, after = [taps_ref[k : k + 1, cols] for k in range(3)]
    up = jnp.where(row == 0, jnp.where(core == 0, 0.0, mate[15:]), pltpu.roll(own, 1, 0))
    down = jnp.where(row == rows - 1, jnp.where(core == 0, mate[:1], 0.0), pltpu.roll(own, rows - 1, 0))
    second = prior * up + here * own + after * down
    second_ref[...] = second.T
    ends_ref[...] = jnp.concatenate(
        [
            jnp.where(core == 0, prior * mate[14:15] + here * mate[15:], second[rows - 1 :]),
            jnp.where(core == 0, second[:1], here * mate[:1] + after * mate[1:2]),
            after * jnp.where(core == 0, own[:1], mate[:1]),
            prior * jnp.where(core == 0, mate[15:], own[rows - 1 :]),
            jnp.zeros((4, channels), F32),
        ],
        0,
    )
    part = ends_ref[:, mine(0)]
    ends = [
        first[:1], value[last:], value[:1], part[:1], part[1:2],
        first_up, first_down, value_up, value_down, part[2:3], part[3:4],
    ]
    fill = jnp.zeros((rows - len(ends) - 1, half), F32)
    place(12, jnp.concatenate(ends + [fill, first[last:]], 0))
    send_ref[...] = wide[...].astype(BF16)


def conv_kernel(got_ref, skip_ref, table_ref, twist_ref, out_ref, buf, wide):
    tok = got_ref.shape[1]
    chips = got_ref.shape[0] // 14
    blocks = 2 * chips
    cos, sin = twist_ref[:, :tok], twist_ref[:, tok:]
    inner = slice(2 * blocks, 2 * blocks + 2 * tok)
    back = slice(2 * blocks + 2 * tok, 3 * blocks + 2 * tok)
    place = lax.broadcasted_iota(jnp.int32, (chips, tok), 0)
    lane = lax.broadcasted_iota(jnp.int32, (chips, tok), 1)
    fft = lax.axis_index("fft")
    owner = fft % 2 * blocks + 2 * (lax.axis_index("blk") * (lax.axis_size("fft") // 2) + fft // 2)

    def left(x, n):
        return pltpu.roll(x, tok - n, 1)

    def take(at):
        return wide[pl.ds(at, chips, stride=14), :]

    def taps(a):
        return jnp.concatenate(
            [jnp.concatenate([take(a + 2 * h + c) for c in range(2)], 1) for h in range(2)], 0
        )

    def spectrum(b):
        parts = []
        for c in range(2):
            lanes = slice(c * tok, (c + 1) * tok)
            re, im = b[:blocks, lanes], b[blocks:, lanes]
            parts.append(jnp.concatenate([re * cos + im * sin, im * cos - re * sin], 1))
        return [dot(part.astype(BF16), table_ref[: 2 * tok, inner]) for part in parts]

    wide[...] = got_ref[...].astype(F32)
    anti = taps(8)
    row = lax.broadcasted_iota(jnp.int32, anti.shape, 0)
    col = lax.broadcasted_iota(jnp.int32, anti.shape, 1)
    anti = jnp.where((row == 0) & (col % tok == 0), 0.0, anti)
    f = spectrum(dot(table_ref[:, : 2 * blocks], jnp.concatenate([taps(4), anti], 0).astype(BF16)))

    signal, end_signal, end_second, skip = [], [], [], []
    at_end = [lane == 0, lane == tok - 1]
    for c in range(2):
        ends = take(12 + c)
        prior = jnp.where(place == 0, 0.0, pltpu.roll(ends, 1, 0))
        after = jnp.where(place == chips - 1, 0.0, pltpu.roll(ends, chips - 1, 0))
        full = ends + left(jnp.where(lane % 2 == 1, after, prior), 6)
        end_signal.append(full * left(full, 2))
        end_second.append(left(full, 4))
        signal.append([jnp.where(at_end[h], end_signal[c], take(2 * h + c)) for h in range(2)])
        index = lax.broadcasted_iota(jnp.int32, skip_ref.shape, 1)
        skip.append(jnp.sum(jnp.where(index == owner + c, skip_ref[...], 0.0), 1, keepdims=True))
    x = jnp.concatenate([jnp.concatenate(part, 0) for part in signal], 1)
    s = spectrum(dot(table_ref[:, :blocks], x.astype(BF16)))

    real, imag = [], []
    for c in range(2):
        sr, si, fr, fi = s[c][:, :tok], s[c][:, tok:], f[c][:, :tok], f[c][:, tok:]
        y = jnp.concatenate([sr * fr - si * fi, sr * fi + si * fr], 1)
        g = dot(y.astype(BF16), table_ref[2 * tok : 4 * tok, inner])
        re, im = g[:, :tok], g[:, tok:]
        real.append(re * cos - im * sin)
        imag.append(re * sin + im * cos)
    e = jnp.concatenate([jnp.concatenate(real, 1), jnp.concatenate(imag, 1)], 0)
    out = dot(jnp.concatenate([table_ref[:blocks, back], table_ref[blocks : 2 * blocks, back]], 1), e.astype(BF16))
    for c in range(2):
        for h in range(2):
            conv = out[h * chips : (h + 1) * chips, c * tok : (c + 1) * tok] + skip[c] * signal[c][h]
            conv = jnp.where(at_end[h], end_second[c] * conv, conv)
            buf[pl.ds(2 * h + c, chips, stride=4), :] = conv
    out_ref[...] = buf[...].astype(BF16)


def last_kernel(conv_ref, second_ref, w_ref, out_ref, buf, sorted_ref):
    channels, rows = conv_ref.shape
    quarter = channels // 4
    buf[...] = conv_ref[...].astype(F32)
    for h in range(2):
        for c in range(2):
            sorted_ref[pl.ds(h * channels // 2 + c, quarter, stride=2), :] = buf[
                pl.ds(2 * h + c, quarter, stride=4), :
            ]
    conv = sorted_ref[...]
    lane = lax.broadcasted_iota(jnp.int32, conv.shape, 1)
    at_end = lane == lax.axis_index("fft") % 2 * (rows - 1)
    gated = jnp.where(at_end, conv, second_ref[...] * conv).astype(BF16)
    out_ref[...] = lax.dot_general(
        gated, w_ref[...], (((0,), (0,)), ((), ())), preferred_element_type=F32
    ).astype(BF16)


def call(kernel, outs, scratch=(), mib=24, cost=0, **specs):
    return pl.pallas_call(
        kernel,
        out_shape=outs,
        scratch_shapes=list(scratch),
        compiler_params=pltpu.CompilerParams(vmem_limit_bytes=mib * 1024 * 1024),
        cost_estimate=pl.CostEstimate(flops=cost, bytes_accessed=0, transcendentals=0) if cost else None,
        **specs,
    )


def exchange(x, groups=None):
    return lax.all_to_all(x, AXES, split_axis=0, concat_axis=0, axis_index_groups=groups, tiled=True)


def body(tokens, w_in, conv_taps, causal_taps, anticausal_taps, skip_gain, w_out):
    rows = tokens.shape[0]
    channels, width = w_out.shape
    count = lax.axis_size(AXES)
    shape = jax.ShapeDtypeStruct
    vmem = pltpu.VMEM
    table = tables(count, rows)

    mates = [(i, i ^ 1) for i in range(count)]
    tok_mate, causal_mate, anti_mate = [lax.ppermute(x, AXES, mates) for x in (tokens, causal_taps, anticausal_taps)]
    twist = call(first_kernel, shape((count, 2 * rows), F32), cost=2 * 10**9)()
    send, second = call(
        front_kernel,
        [shape((7 * count, rows), BF16), shape((channels, rows), F32)],
        [
            vmem((2 * rows, tokens.shape[1]), BF16),
            vmem((8, channels), F32),
            vmem((channels // 2, rows), F32),
            vmem((7 * count, rows), F32),
        ],
    )(twist, tokens, tok_mate, w_in, conv_taps, causal_taps, causal_mate, anticausal_taps, anti_mate)
    cores = [list(range(core, count, 2)) for core in range(2)]
    got = exchange(send.reshape(-1, 2, rows), cores).reshape(send.shape)

    conv = call(
        conv_kernel,
        shape((channels, rows), BF16),
        [vmem((channels, rows), F32), vmem((7 * count, rows), F32)],
    )(got, skip_gain[None], table, twist)
    conv = exchange(conv)
    return call(last_kernel, shape((rows, width), BF16), [vmem((channels, rows), F32)] * 2)(conv, second, w_out)


def solution(mesh):
    rows = P(AXES, None)
    in_specs = (rows, P(), P(), rows, rows, P(), P())
    return jax.shard_map(body, mesh=mesh, in_specs=in_specs, out_specs=rows, check_vma=False)
```

time: 60.1 us -> 60.4 us (level)
  starting transfers between devices: 0 us -> 3.82 us
  blocking collectives: 54.4 us -> 51.7 us
  local copies, waits for them, and re-layouts: 1.54 us -> 0.04 us
  waiting for transfers between devices: 0 us -> 0.7 us
    ppermute x0 -> x3, starting transfers between devices: none -> 3.82 us  [body(): lax.ppermute(x, AXES, mates)]
    all_to_all x2, blocking collectives: 54.4 us -> 51.7 us  [exchange(): lax.all_to_all(x, AXES, split_axis=0, concat_axis=0, axis_index_groups=gr...]
    unnamed x16, local copies, waits for them, and re-layouts: 1.54 us -> 0.04 us
    ppermute x0 -> x3, waiting for transfers between devices: none -> 0.7 us  [body(): lax.ppermute(x, AXES, mates)]
  transfers between devices with their start and end apart: 0 -> 3, of which waited for: 0 -> 2; matrix products, arithmetic and copies ran while one was open for 0% -> 0% of each run, Pallas kernels for 0% -> 1%
where the time goes in v5:
time: 60.4 us; the launch traced here: 60.3 us
  blocking collectives  51.7 us (86%)
  Pallas kernels  3.94 us (7%)
  starting transfers between devices  3.82 us (6%)
  waiting for transfers between devices  0.7 us (1%)
    all_to_all x2, blocking collectives, exchange(): lax.all_to_all(x, AXES, split_axis=0, concat_axis=0, axis_index_groups=gr...  51.7 us
    ppermute x3, starting transfers between devices, body(): lax.ppermute(x, AXES, mates)  3.82 us
    pallas_call x1, Pallas kernels, body(): call(conv_kernel, shape((channels, rows), BF16), [vmem((channels, rows),...  1.28 us
  transfers between devices with their start and end apart: 3, of which 2 were waited for; matrix products, arithmetic and copies ran while one was open for 0% of the time, Pallas kernels for 1%

profile of v5, /device:TPU:1, one launch (start us, length us, event | category | flops | bytes accessed | tf_op | source)
XLA Modules:
  0.0 60.3 jit_solution(9991659686094693471)
XLA Ops:
  0.0 0.0 copy-start.3
  0.0 0.0 copy-start.4
  0.0 0.0 copy-start.5
  0.0 0.0 copy-start.6
  0.0 0.0 copy-start
  0.0 3.3 %collective-permute-start = (bf16[128,1024]{1,0:T(8,128)(2,1)}, bf16[128,1024]{1,0:T(8,128)(2,1)S(1)}, u32[]{:S(2)}, u32[]{:S(2)}) collective-permute-start(bf16[128,1024]{1,0:T(8,128)(2,1)} %tok_ref.1), channel_id=1, source_target_pairs={{0,1},{1,0},{2,3},{3,2},{4,5},{5,4},{6,7},{7,6},{8,9},{9,8},{10,11... | collective-permute-start | bytes 786440 | tf_op jit(solution)/shard_map/ppermute | solution.py:229
  3.3 0.1 collective-permute-start.1
  3.4 0.4 collective-permute-start.2
  3.9 0.5 shard_map.82._.twist_ref
  4.4 0.0 copy-start.1
  4.4 0.0 copy-start.7
  4.4 0.0 copy-start.2
  4.4 0.5 collective-permute-done.1.causal_mate_ref
  4.9 0.2 collective-permute-done.2.anti_mate_ref
  5.1 0.0 collective-permute-done.tok_mate_ref
  5.1 0.0 copy-done.3
  5.1 0.0 copy-done.4
  5.1 0.0 copy-done.5
  5.1 0.0 copy-done.6
  5.1 0.0 copy-done
  5.1 1.1 %shard_map.83 = (bf16[1792,128]{1,0:T(8,128)(2,1)S(1)}, f32[512,128]{1,0:T(8,128)S(1)}) custom-call(f32[256,256]{1,0:T(8,128)S(1)} %shard_map.82._.twist_ref, bf16[128,1024]{1,0:T(8,128)(2,1)S(1)} %copy-done.3, bf16[128,1024]{1,0:T(8,128)(2,1)S(1)} %collective-permute-done.tok_mate_ref, bf16[1024,1536]{1,0:T(8,128)(2,1)S(1)} %copy-done, ...), custom_call_target="tpu_custom_call" | custom-call | tf_op jit(solution)/shard_map/pallas_call | solution.py:231
  6.2 31.1 %all_to_all.16 = bf16[896,2,128]{2,1,0:T(2,128)(2,1)S(1)} all-to-all(bf16[896,2,128]{2,1,0:T(2,128)(2,1)S(1)} %bitcast.8), channel_id=1, replica_groups={{0,2,4,6,8,10,12,14,16,18,20,22,24,26,28,30,32,34,36,38,40,42,44,46,48,..., dimensions={0} | all-to-all | bytes 917504 | tf_op jit(solution)/shard_map/all_to_all | solution.py:217
  37.3 0.0 copy-done.1
  37.3 0.0 copy-done.7
  37.3 1.3 %shard_map.84 = bf16[512,128]{1,0:T(8,128)(2,1)S(1)} custom-call(bf16[1792,128]{1,0:T(8,128)(2,1)S(1)} %bitcast.5, f32[1,512]{1,0:T(1,128)S(1)} %bitcast.9, bf16[512,1024]{1,0:T(8,128)(2,1)S(1)} %copy-done.1, f32[256,256]{1,0:T(8,128)S(1)} %shard_map.82._.twist_ref), custom_call_target="tpu_custom_call" | custom-call | tf_op jit(solution)/shard_map/pallas_call | solution.py:244
  38.6 20.5 %all_to_all.17 = bf16[256,2,128]{2,1,0:T(2,128)(2,1)S(1)} all-to-all(bf16[256,2,128]{2,1,0:T(2,128)(2,1)S(1)} %bitcast.6), channel_id=1, replica_groups=mesh['blk'=8,'fft'=32] {'blk','fft'}, dimensions={0} | all-to-all | bytes 262144 | tf_op jit(solution)/shard_map/all_to_all | solution.py:217
  59.2 0.0 copy-done.2
  59.2 1.1 %shard_map.85 = bf16[128,1024]{1,0:T(8,128)(2,1)} custom-call(bf16[512,128]{1,0:T(8,128)(2,1)S(1)} %bitcast.7, f32[512,128]{1,0:T(8,128)S(1)} %get-tuple-element.8.second_ref, bf16[512,1024]{1,0:T(8,128)(2,1)S(1)} %copy-done.2), custom_call_target="tpu_custom_call" | custom-call | tf_op jit(solution)/shard_map/pallas_call | solution.py:250
Async XLA Ops:
  0.0 5.1 %copy-start.3 = (bf16[128,1024]{1,0:T(8,128)(2,1)S(1)}, bf16[128,1024]{1,0:T(8,128)(2,1)}, u32[]{:S(2)}) copy-start(bf16[128,1024]{1,0:T(8,128)(2,1)} %tok_ref.1) | copy-start | bytes 786436
  0.0 5.1 %copy-start.4 = (bf16[128,512]{1,0:T(8,128)(2,1)S(1)}, bf16[128,512]{1,0:T(8,128)(2,1)}, u32[]{:S(2)}) copy-start(bf16[128,512]{1,0:T(8,128)(2,1)} %causal_ref.1) | copy-start | bytes 393220
  0.0 5.1 %copy-start.5 = (bf16[128,512]{1,0:T(8,128)(2,1)S(1)}, bf16[128,512]{1,0:T(8,128)(2,1)}, u32[]{:S(2)}) copy-start(bf16[128,512]{1,0:T(8,128)(2,1)} %anti_ref.1) | copy-start | bytes 393220
  0.0 5.1 %copy-start.6 = (f32[3,1536]{1,0:T(4,128)S(1)}, f32[3,1536]{1,0:T(4,128)}, u32[]{:S(2)}) copy-start(f32[3,1536]{1,0:T(4,128)} %taps_ref.1) | copy-start | bytes 55300
  0.0 5.1 %copy-start = (bf16[1024,1536]{1,0:T(8,128)(2,1)S(1)}, bf16[1024,1536]{1,0:T(8,128)(2,1)}, u32[]{:S(2)}) copy-start(bf16[1024,1536]{1,0:T(8,128)(2,1)} %w_ref.2) | copy-start | bytes 9437188
  0.0 5.1 %collective-permute-start = (bf16[128,1024]{1,0:T(8,128)(2,1)}, bf16[128,1024]{1,0:T(8,128)(2,1)S(1)}, u32[]{:S(2)}, u32[]{:S(2)}) collective-permute-start(bf16[128,1024]{1,0:T(8,128)(2,1)} %tok_ref.1), channel_id=1, source_target_pairs={{0,1},{1,0},{2,3},{3,2},{4,5},{5,4},{6,7},{7,6},{8,9},{9,8},{10,11... | collective-permute-start | bytes 786440 | tf_op jit(solution)/shard_map/ppermute | solution.py:229
  3.3 1.6 %collective-permute-start.1 = (bf16[128,512]{1,0:T(8,128)(2,1)}, bf16[128,512]{1,0:T(8,128)(2,1)S(1)}, u32[]{:S(2)}, u32[]{:S(2)}) collective-permute-start(bf16[128,512]{1,0:T(8,128)(2,1)} %causal_ref.1), channel_id=1, source_target_pairs={{0,1},{1,0},{2,3},{3,2},{4,5},{5,4},{6,7},{7,6},{8,9},{9,8},{10,11... | collective-permute-start | bytes 393224 | tf_op jit(solution)/shard_map/ppermute | solution.py:229
  3.4 1.6 %collective-permute-start.2 = (bf16[128,512]{1,0:T(8,128)(2,1)}, bf16[128,512]{1,0:T(8,128)(2,1)S(1)}, u32[]{:S(2)}, u32[]{:S(2)}) collective-permute-start(bf16[128,512]{1,0:T(8,128)(2,1)} %anti_ref.1), channel_id=1, source_target_pairs={{0,1},{1,0},{2,3},{3,2},{4,5},{5,4},{6,7},{7,6},{8,9},{9,8},{10,11... | collective-permute-start | bytes 393224 | tf_op jit(solution)/shard_map/ppermute | solution.py:229
  4.4 33.0 %copy-start.1 = (bf16[512,1024]{1,0:T(8,128)(2,1)S(1)}, bf16[512,1024]{1,0:T(8,128)(2,1)}, u32[]{:S(2)}) copy-start(bf16[512,1024]{1,0:T(8,128)(2,1)} %constant.2.clone.table_ref) | copy-start | bytes 3145732
  4.4 33.0 %copy-start.7 = (f32[512]{0:T(512)S(1)}, f32[512]{0:T(512)}, u32[]{:S(2)}) copy-start(f32[512]{0:T(512)} %param.13) | copy-start | bytes 6148
  4.4 54.8 %copy-start.2 = (bf16[512,1024]{1,0:T(8,128)(2,1)S(1)}, bf16[512,1024]{1,0:T(8,128)(2,1)}, u32[]{:S(2)}) copy-start(bf16[512,1024]{1,0:T(8,128)(2,1)} %w_ref.3) | copy-start | bytes 3145732

commit v6 on v4

--- a/solution.py
+++ b/solution.py
@@ -11,6 +11,7 @@
 AXES = ("blk", "fft")
 F32 = jnp.float32
 BF16 = jnp.bfloat16
+MESSAGE, ROW = 25, 3
 
 
 def tables(blocks, tok):
@@ -54,7 +55,7 @@
     def place(a, block):
         buf[...] = block.T
         for c in range(2):
-            wide[pl.ds(2 * a + c, half, stride=8), :] = buf[pl.ds(c, half, stride=2), :]
+            wide[pl.ds(ROW * (2 * a + c), half, stride=MESSAGE), :] = buf[pl.ds(c, half, stride=2), :]
 
     def short(i):
         proj = dot(tok_ref[...], w_ref[:, slab(i)]).astype(BF16).astype(F32)
@@ -80,7 +81,9 @@
     ]
     fill = jnp.zeros((rows - len(ends) - 1, channels), F32)
     place(3, jnp.concatenate(ends + [fill, first[last:]], 0))
-    send_ref[...] = wide[...].astype(BF16)
+    for i in range(0, half, 2):
+        pair = [wide[pl.ds(MESSAGE * (i + k), 8, stride=ROW), :] for k in range(2)]
+        send_ref[8 * i : 8 * i + 16, :] = jnp.concatenate(pair, 0).astype(BF16)
 
 
 def conv_kernel(got_ref, table_ref, twist_ref, out_ref, buf, wide):
@@ -97,7 +100,7 @@
         return pltpu.roll(x, tok - n, 1)
 
     def take(a, c):
-        return wide[pl.ds(2 * a + c, blocks, stride=8), :]
+        return wide[pl.ds(ROW * (2 * a + c), blocks, stride=MESSAGE), :]
 
     def spectrum(b):
         parts = []
@@ -107,7 +110,9 @@
             parts.append(jnp.concatenate([re * cos + im * sin, im * cos - re * sin], 1))
         return [dot(part.astype(BF16), table_ref[: 2 * tok, inner]) for part in parts]
 
-    wide[...] = got_ref[...].astype(F32)
+    got = got_ref[...].astype(F32)
+    for i in range(blocks):
+        wide[pl.ds(MESSAGE * i, 8, stride=ROW), :] = got[8 * i : 8 * i + 8]
     causal = jnp.concatenate([take(1, 0), take(1, 1)], 1)
     anti = jnp.concatenate(
         [jnp.where((place == 0) & (lane == 0), 0.0, take(2, c)) for c in range(2)], 1
@@ -181,14 +186,14 @@
     send, second, direct = call(
         front_kernel,
         [shape((4 * channels, rows), BF16), shape((channels, rows), F32), shape((channels, rows), F32)],
-        [vmem((channels, rows), F32), vmem((4 * channels, rows), F32)],
+        [vmem((channels, rows), F32), vmem((MESSAGE * (count + 1), rows), F32)],
     )(twist, *staged)
     got = exchange(send.reshape(count, 8, rows)).reshape(send.shape)
 
     conv = call(
         conv_kernel,
         shape((channels, rows), BF16),
-        [vmem((channels, rows), F32), vmem((4 * channels, rows), F32)],
+        [vmem((channels, rows), F32), vmem((MESSAGE * (count + 1), rows), F32)],
     )(got, table, twist)
     conv = exchange(conv)
     return call(last_kernel, shape((rows, width), BF16))(conv, second, direct, w_out)

time: 60.1 us -> 60 us (level)
  no operation moved by 1% of the time
where the time goes in v6:
time: 60 us; the launch traced here: 59.8 us
  blocking collectives  54.4 us (91%)
  Pallas kernels  3.89 us (6%)
  local copies, waits for them, and re-layouts  1.54 us (3%)
    all_to_all x2, blocking collectives, exchange(): return lax.all_to_all(x, AXES, split_axis=0, concat_axis=0, tiled=True)  54.4 us
    unnamed x16, local copies, waits for them, and re-layouts  1.54 us
    pallas_call x1, Pallas kernels, body(): call(conv_kernel, shape((channels, rows), BF16), [vmem((channels, rows),...  1.32 us

profile of v6, /device:TPU:1, one launch (start us, length us, event | category | flops | bytes accessed | tf_op | source)
XLA Modules:
  0.0 59.8 jit_solution(5121330456060835686)
XLA Ops:
  0.0 0.0 copy-start.7
  0.0 0.0 copy-start.5
  0.0 0.0 copy-start.4
  0.0 0.0 copy-start.6
  0.0 0.0 copy-start
  0.0 0.0 copy-start.3
  0.0 0.5 shard_map.82._.twist_ref
  0.5 0.0 copy-start.2
  0.6 0.1 copy-done.7
  0.7 0.2 copy-done.5
  0.9 0.1 copy-done.4
  1.0 0.0 copy-done.6
  1.0 1.1 %copy-done = bf16[1024,1536]{1,0:T(8,128)(2,1)S(1)} copy-done((bf16[1024,1536]{1,0:T(8,128)(2,1)S(1)}, bf16[1024,1536]{1,0:T(8,128)(2,1)}, u32[]{:S(2)}) %copy-start) | copy-done | bytes 3145752
  2.1 0.0 copy-done.3
  2.1 0.0 copy-start.1
  2.1 1.0 %shard_map.83 = (bf16[2048,128]{1,0:T(8,128)(2,1)S(1)}, f32[512,128]{1,0:T(8,128)S(1)}, f32[512,128]{1,0:T(8,128)S(1)}) custom-call(f32[256,256]{1,0:T(8,128)S(1)} %shard_map.82._.twist_ref, bf16[128,1024]{1,0:T(8,128)(2,1)S(1)} %copy-done.3, bf16[1024,1536]{1,0:T(8,128)(2,1)S(1)} %copy-done, f32[3,1536]{1,0:T(4,128)S(1)} %copy-done.6, ...), custom_call_target="tpu_custom_call" | custom-call | tf_op jit(solution)/shard_map/pallas_call | solution.py:186
  3.1 35.4 %all_to_all.16 = bf16[256,8,128]{2,1,0:T(8,128)(2,1)S(1)} all-to-all(bf16[256,8,128]{2,1,0:T(8,128)(2,1)S(1)} %bitcast.6), channel_id=1, replica_groups=mesh['blk'=8,'fft'=32] {'blk','fft'}, dimensions={0} | all-to-all | bytes 1048576 | tf_op jit(solution)/shard_map/all_to_all | solution.py:173
  38.5 0.0 copy-done.2
  38.5 1.3 %shard_map.84 = bf16[512,128]{1,0:T(8,128)(2,1)S(1)} custom-call(bf16[2048,128]{1,0:T(8,128)(2,1)S(1)} %bitcast.5, bf16[512,1024]{1,0:T(8,128)(2,1)S(1)} %copy-done.2, f32[256,256]{1,0:T(8,128)S(1)} %shard_map.82._.twist_ref), custom_call_target="tpu_custom_call" | custom-call | tf_op jit(solution)/shard_map/pallas_call | solution.py:193
  39.9 18.9 %all_to_all.17 = bf16[256,2,128]{2,1,0:T(2,128)(2,1)S(1)} all-to-all(bf16[256,2,128]{2,1,0:T(2,128)(2,1)S(1)} %bitcast.8), channel_id=1, replica_groups=mesh['blk'=8,'fft'=32] {'blk','fft'}, dimensions={0} | all-to-all | bytes 262144 | tf_op jit(solution)/shard_map/all_to_all | solution.py:173
  58.8 0.0 copy-done.1
  58.8 1.1 %shard_map.85 = bf16[128,1024]{1,0:T(8,128)(2,1)} custom-call(bf16[512,128]{1,0:T(8,128)(2,1)S(1)} %bitcast.7, f32[512,128]{1,0:T(8,128)S(1)} %get-tuple-element.9.second_ref, f32[512,128]{1,0:T(8,128)S(1)} %get-tuple-element.10.direct_ref, bf16[512,1024]{1,0:T(8,128)(2,1)S(1)} %copy-done.1), custom_call_target="tpu_custom_call" | custom-call | tf_op jit(solution)/shard_map/pallas_call | solution.py:199
Async XLA Ops:
  0.0 0.7 %copy-start.7 = (f32[512]{0:T(512)S(1)}, f32[512]{0:T(512)}, u32[]{:S(2)}) copy-start(f32[512]{0:T(512)} %param.13) | copy-start | bytes 6148
  0.0 0.9 %copy-start.5 = (bf16[128,512]{1,0:T(8,128)(2,1)S(1)}, bf16[128,512]{1,0:T(8,128)(2,1)}, u32[]{:S(2)}) copy-start(bf16[128,512]{1,0:T(8,128)(2,1)} %anti_ref.1) | copy-start | bytes 393220
  0.0 1.0 %copy-start.4 = (bf16[128,512]{1,0:T(8,128)(2,1)S(1)}, bf16[128,512]{1,0:T(8,128)(2,1)}, u32[]{:S(2)}) copy-start(bf16[128,512]{1,0:T(8,128)(2,1)} %causal_ref.1) | copy-start | bytes 393220
  0.0 1.0 %copy-start.6 = (f32[3,1536]{1,0:T(4,128)S(1)}, f32[3,1536]{1,0:T(4,128)}, u32[]{:S(2)}) copy-start(f32[3,1536]{1,0:T(4,128)} %taps_ref.1) | copy-start | bytes 55300
  0.0 2.1 %copy-start = (bf16[1024,1536]{1,0:T(8,128)(2,1)S(1)}, bf16[1024,1536]{1,0:T(8,128)(2,1)}, u32[]{:S(2)}) copy-start(bf16[1024,1536]{1,0:T(8,128)(2,1)} %w_ref.2) | copy-start | bytes 9437188
  0.0 2.0 %copy-start.3 = (bf16[128,1024]{1,0:T(8,128)(2,1)S(1)}, bf16[128,1024]{1,0:T(8,128)(2,1)}, u32[]{:S(2)}) copy-start(bf16[128,1024]{1,0:T(8,128)(2,1)} %tok_ref.1) | copy-start | bytes 786436
  0.5 38.0 %copy-start.2 = (bf16[512,1024]{1,0:T(8,128)(2,1)S(1)}, bf16[512,1024]{1,0:T(8,128)(2,1)}, u32[]{:S(2)}) copy-start(bf16[512,1024]{1,0:T(8,128)(2,1)} %constant.2.clone.table_ref) | copy-start | bytes 3145732
  2.1 56.7 %copy-start.1 = (bf16[512,1024]{1,0:T(8,128)(2,1)S(1)}, bf16[512,1024]{1,0:T(8,128)(2,1)}, u32[]{:S(2)}) copy-start(bf16[512,1024]{1,0:T(8,128)(2,1)} %w_ref.3) | copy-start | bytes 3145732

commit v7 on v6

--- a/solution.py
+++ b/solution.py
@@ -41,8 +41,8 @@
 
 
 def front_kernel(
-    _, tok_ref, w_ref, taps_ref, skip_ref, causal_ref, anti_ref,
-    send_ref, second_ref, direct_ref, buf, wide,
+    _, tok_ref, w_ref, taps_ref, causal_ref, anti_ref,
+    send_ref, second_ref, buf, wide,
 ):
     rows = tok_ref.shape[0]
     channels = causal_ref.shape[1]
@@ -70,14 +70,12 @@
     value, value_up, value_down = short(2)
     signal = first * value
     place(0, signal)
-    direct_ref[...] = (skip_ref[...] * signal).T
     second, second_up, second_down = short(1)
     second_ref[...] = second.T
     last = rows - 1
     ends = [
         first[:1], value[last:], value[:1], second[last:], second[:1],
         first_up, first_down, value_up, value_down, second_up, second_down,
-        skip_ref[...], skip_ref[...],
     ]
     fill = jnp.zeros((rows - len(ends) - 1, channels), F32)
     place(3, jnp.concatenate(ends + [fill, first[last:]], 0))
@@ -86,7 +84,7 @@
         send_ref[8 * i : 8 * i + 16, :] = jnp.concatenate(pair, 0).astype(BF16)
 
 
-def conv_kernel(got_ref, table_ref, twist_ref, out_ref, buf, wide):
+def conv_kernel(got_ref, skip_ref, table_ref, twist_ref, out_ref, buf, wide):
     tok = got_ref.shape[1]
     blocks = got_ref.shape[0] // 8
     cos, sin = twist_ref[:, :tok], twist_ref[:, tok:]
@@ -106,7 +104,7 @@
         parts = []
         for c in range(2):
             lanes = slice(c * tok, (c + 1) * tok)
-            re, im = b[:blocks, lanes], b[blocks:, lanes]
+            re, im = b[0][:, lanes], b[1][:, lanes]
             parts.append(jnp.concatenate([re * cos + im * sin, im * cos - re * sin], 1))
         return [dot(part.astype(BF16), table_ref[: 2 * tok, inner]) for part in parts]
 
@@ -117,19 +115,22 @@
     anti = jnp.concatenate(
         [jnp.where((place == 0) & (lane == 0), 0.0, take(2, c)) for c in range(2)], 1
     )
-    f = spectrum(dot(table_ref[:, : 2 * blocks], jnp.concatenate([causal, anti], 0).astype(BF16)))
-
-    signal, end_signal, end_second, end_skip = [], [], [], []
+    taps = jnp.concatenate([causal, anti], 0).astype(BF16)
+    f = spectrum([dot(table_ref[i * blocks : (i + 1) * blocks, : 2 * blocks], taps) for i in range(2)])
+
+    signal, end_second, skip = [], [], []
+    device = lax.axis_index("blk") * lax.axis_size("fft") + lax.axis_index("fft")
+    channel = lax.broadcasted_iota(jnp.int32, skip_ref.shape, 1)
     for c in range(2):
         ends = take(3, c)
         prior = jnp.where(place == 0, 0.0, pltpu.roll(ends, 1, 0))
         after = jnp.where(place == blocks - 1, 0.0, pltpu.roll(ends, blocks - 1, 0))
         full = ends + left(jnp.where(lane % 2 == 1, after, prior), 6)
-        end_signal.append(full * left(full, 2))
         end_second.append(left(full, 4))
-        end_skip.append(left(ends, 12))
-        signal.append(jnp.where(at_end, end_signal[c], take(0, c)))
-    s = spectrum(dot(table_ref[:, :blocks], jnp.concatenate(signal, 1).astype(BF16)))
+        signal.append(jnp.where(at_end, full * left(full, 2), take(0, c)))
+        skip.append(jnp.sum(jnp.where(channel == 2 * device + c, skip_ref[...], 0.0), 1, keepdims=True))
+    x = jnp.concatenate(signal, 1).astype(BF16)
+    s = spectrum([dot(table_ref[i * blocks : (i + 1) * blocks, :blocks], x) for i in range(2)])
 
     real, imag = [], []
     for c in range(2):
@@ -142,17 +143,16 @@
     e = jnp.concatenate([jnp.concatenate(real, 1), jnp.concatenate(imag, 1)], 0)
     out = dot(jnp.concatenate([table_ref[:blocks, back], table_ref[blocks : 2 * blocks, back]], 1), e.astype(BF16))
     for c in range(2):
-        conv = out[:, c * tok : (c + 1) * tok]
-        gated = end_second[c] * (conv + end_skip[c] * end_signal[c])
-        buf[pl.ds(c, blocks, stride=2), :] = jnp.where(at_end, gated, conv)
+        conv = out[:, c * tok : (c + 1) * tok] + skip[c] * signal[c]
+        buf[pl.ds(c, blocks, stride=2), :] = jnp.where(at_end, end_second[c] * conv, conv)
     out_ref[...] = buf[...].astype(BF16)
 
 
-def last_kernel(conv_ref, second_ref, direct_ref, w_ref, out_ref):
+def last_kernel(conv_ref, second_ref, w_ref, out_ref):
     conv = conv_ref[...].astype(F32)
     lane = lax.broadcasted_iota(jnp.int32, conv.shape, 1)
     at_end = (lane == 0) | (lane == conv.shape[1] - 1)
-    gated = jnp.where(at_end, conv, second_ref[...] * (conv + direct_ref[...])).astype(BF16)
+    gated = jnp.where(at_end, conv, second_ref[...] * conv).astype(BF16)
     out_ref[...] = lax.dot_general(
         gated, w_ref[...], (((0,), (0,)), ((), ())), preferred_element_type=F32
     ).astype(BF16)
@@ -181,11 +181,11 @@
     vmem = pltpu.VMEM
     table = tables(count, rows)
 
-    staged = (tokens, w_in, conv_taps, skip_gain[None], causal_taps, anticausal_taps)
+    staged = (tokens, w_in, conv_taps, causal_taps, anticausal_taps)
     twist = call(first_kernel, shape((count, 2 * rows), F32), cost=2 * 10**9)()
-    send, second, direct = call(
+    send, second = call(
         front_kernel,
-        [shape((4 * channels, rows), BF16), shape((channels, rows), F32), shape((channels, rows), F32)],
+        [shape((4 * channels, rows), BF16), shape((channels, rows), F32)],
         [vmem((channels, rows), F32), vmem((MESSAGE * (count + 1), rows), F32)],
     )(twist, *staged)
     got = exchange(send.reshape(count, 8, rows)).reshape(send.shape)
@@ -194,9 +194,9 @@
         conv_kernel,
         shape((channels, rows), BF16),
         [vmem((channels, rows), F32), vmem((MESSAGE * (count + 1), rows), F32)],
-    )(got, table, twist)
+    )(got, skip_gain[None], table, twist)
     conv = exchange(conv)
-    return call(last_kernel, shape((rows, width), BF16))(conv, second, direct, w_out)
+    return call(last_kernel, shape((rows, width), BF16))(conv, second, w_out)
 
 
 def solution(mesh):

time: 60 us -> 59.8 us (level)
  no operation moved by 1% of the time
where the time goes in v7:
time: 59.8 us; the launch traced here: 59.7 us
  blocking collectives  54.4 us (91%)
  Pallas kernels  3.75 us (6%)
  local copies, waits for them, and re-layouts  1.55 us (3%)
    all_to_all x2, blocking collectives, exchange(): return lax.all_to_all(x, AXES, split_axis=0, concat_axis=0, tiled=True)  54.4 us
    unnamed x16, local copies, waits for them, and re-layouts  1.55 us
    pallas_call x1, Pallas kernels, body(): call(conv_kernel, shape((channels, rows), BF16), [vmem((channels, rows),...  1.24 us

profile of v7, /device:TPU:1, one launch (start us, length us, event | category | flops | bytes accessed | tf_op | source)
XLA Modules:
  0.0 59.7 jit_solution(12942606492476175831)
XLA Ops:
  0.0 0.0 copy-start.5
  0.0 0.0 copy-start.4
  0.0 0.0 copy-start.6
  0.0 0.0 copy-start
  0.0 0.0 copy-start.3
  0.0 0.5 shard_map.82._.twist_ref
  0.5 0.4 copy-done.5
  0.9 0.1 copy-done.4
  1.0 0.0 copy-done.6
  1.0 1.1 %copy-done = bf16[1024,1536]{1,0:T(8,128)(2,1)S(1)} copy-done((bf16[1024,1536]{1,0:T(8,128)(2,1)S(1)}, bf16[1024,1536]{1,0:T(8,128)(2,1)}, u32[]{:S(2)}) %copy-start) | copy-done | bytes 3145752
  2.1 0.0 copy-done.3
  2.1 0.0 copy-start.1
  2.1 0.0 copy-start.7
  2.1 0.0 copy-start.2
  2.1 1.0 %shard_map.83 = (bf16[2048,128]{1,0:T(8,128)(2,1)S(1)}, f32[512,128]{1,0:T(8,128)S(1)}) custom-call(f32[256,256]{1,0:T(8,128)S(1)} %shard_map.82._.twist_ref, bf16[128,1024]{1,0:T(8,128)(2,1)S(1)} %copy-done.3, bf16[1024,1536]{1,0:T(8,128)(2,1)S(1)} %copy-done, f32[3,1536]{1,0:T(4,128)S(1)} %copy-done.6, bf16[128,512]{1,0:T(8,128)(2,1)S(1)} %copy-done.4, ...), custom_call_target="tpu_custom_call" | custom-call | tf_op jit(solution)/shard_map/pallas_call | solution.py:186
  3.0 35.4 %all_to_all.16 = bf16[256,8,128]{2,1,0:T(8,128)(2,1)S(1)} all-to-all(bf16[256,8,128]{2,1,0:T(8,128)(2,1)S(1)} %bitcast.7), channel_id=1, replica_groups=mesh['blk'=8,'fft'=32] {'blk','fft'}, dimensions={0} | all-to-all | bytes 1048576 | tf_op jit(solution)/shard_map/all_to_all | solution.py:173
  38.5 0.0 copy-done.1
  38.5 0.0 copy-done.7
  38.5 1.2 %shard_map.84 = bf16[512,128]{1,0:T(8,128)(2,1)S(1)} custom-call(bf16[2048,128]{1,0:T(8,128)(2,1)S(1)} %bitcast.5, f32[1,512]{1,0:T(1,128)S(1)} %bitcast.9, bf16[512,1024]{1,0:T(8,128)(2,1)S(1)} %copy-done.1, f32[256,256]{1,0:T(8,128)S(1)} %shard_map.82._.twist_ref), custom_call_target="tpu_custom_call" | custom-call | tf_op jit(solution)/shard_map/pallas_call | solution.py:193
  39.7 18.9 %all_to_all.17 = bf16[256,2,128]{2,1,0:T(2,128)(2,1)S(1)} all-to-all(bf16[256,2,128]{2,1,0:T(2,128)(2,1)S(1)} %bitcast.6), channel_id=1, replica_groups=mesh['blk'=8,'fft'=32] {'blk','fft'}, dimensions={0} | all-to-all | bytes 262144 | tf_op jit(solution)/shard_map/all_to_all | solution.py:173
  58.7 0.0 copy-done.2
  58.7 1.0 %shard_map.85 = bf16[128,1024]{1,0:T(8,128)(2,1)} custom-call(bf16[512,128]{1,0:T(8,128)(2,1)S(1)} %bitcast.8, f32[512,128]{1,0:T(8,128)S(1)} %get-tuple-element.8.second_ref, bf16[512,1024]{1,0:T(8,128)(2,1)S(1)} %copy-done.2), custom_call_target="tpu_custom_call" | custom-call | tf_op jit(solution)/shard_map/pallas_call | solution.py:199
Async XLA Ops:
  0.0 0.9 %copy-start.5 = (bf16[128,512]{1,0:T(8,128)(2,1)S(1)}, bf16[128,512]{1,0:T(8,128)(2,1)}, u32[]{:S(2)}) copy-start(bf16[128,512]{1,0:T(8,128)(2,1)} %anti_ref.1) | copy-start | bytes 393220
  0.0 1.0 %copy-start.4 = (bf16[128,512]{1,0:T(8,128)(2,1)S(1)}, bf16[128,512]{1,0:T(8,128)(2,1)}, u32[]{:S(2)}) copy-start(bf16[128,512]{1,0:T(8,128)(2,1)} %causal_ref.1) | copy-start | bytes 393220
  0.0 1.0 %copy-start.6 = (f32[3,1536]{1,0:T(4,128)S(1)}, f32[3,1536]{1,0:T(4,128)}, u32[]{:S(2)}) copy-start(f32[3,1536]{1,0:T(4,128)} %taps_ref.1) | copy-start | bytes 55300
  0.0 2.1 %copy-start = (bf16[1024,1536]{1,0:T(8,128)(2,1)S(1)}, bf16[1024,1536]{1,0:T(8,128)(2,1)}, u32[]{:S(2)}) copy-start(bf16[1024,1536]{1,0:T(8,128)(2,1)} %w_ref.2) | copy-start | bytes 9437188
  0.0 2.0 %copy-start.3 = (bf16[128,1024]{1,0:T(8,128)(2,1)S(1)}, bf16[128,1024]{1,0:T(8,128)(2,1)}, u32[]{:S(2)}) copy-start(bf16[128,1024]{1,0:T(8,128)(2,1)} %tok_ref.1) | copy-start | bytes 786436
  2.1 36.4 %copy-start.1 = (bf16[512,1024]{1,0:T(8,128)(2,1)S(1)}, bf16[512,1024]{1,0:T(8,128)(2,1)}, u32[]{:S(2)}) copy-start(bf16[512,1024]{1,0:T(8,128)(2,1)} %constant.2.clone.table_ref) | copy-start | bytes 3145732
  2.1 36.4 %copy-start.7 = (f32[512]{0:T(512)S(1)}, f32[512]{0:T(512)}, u32[]{:S(2)}) copy-start(f32[512]{0:T(512)} %param.13) | copy-start | bytes 6148
  2.1 56.6 %copy-start.2 = (bf16[512,1024]{1,0:T(8,128)(2,1)S(1)}, bf16[512,1024]{1,0:T(8,128)(2,1)}, u32[]{:S(2)}) copy-start(bf16[512,1024]{1,0:T(8,128)(2,1)} %w_ref.3) | copy-start | bytes 3145732

commit v8 on v6

--- a/solution.py
+++ b/solution.py
@@ -106,7 +106,7 @@
         parts = []
         for c in range(2):
             lanes = slice(c * tok, (c + 1) * tok)
-            re, im = b[:blocks, lanes], b[blocks:, lanes]
+            re, im = b[0][:, lanes], b[1][:, lanes]
             parts.append(jnp.concatenate([re * cos + im * sin, im * cos - re * sin], 1))
         return [dot(part.astype(BF16), table_ref[: 2 * tok, inner]) for part in parts]
 
@@ -117,7 +117,8 @@
     anti = jnp.concatenate(
         [jnp.where((place == 0) & (lane == 0), 0.0, take(2, c)) for c in range(2)], 1
     )
-    f = spectrum(dot(table_ref[:, : 2 * blocks], jnp.concatenate([causal, anti], 0).astype(BF16)))
+    taps = jnp.concatenate([causal, anti], 0).astype(BF16)
+    f = spectrum([dot(table_ref[i * blocks : (i + 1) * blocks, : 2 * blocks], taps) for i in range(2)])
 
     signal, end_signal, end_second, end_skip = [], [], [], []
     for c in range(2):
@@ -129,7 +130,8 @@
         end_second.append(left(full, 4))
         end_skip.append(left(ends, 12))
         signal.append(jnp.where(at_end, end_signal[c], take(0, c)))
-    s = spectrum(dot(table_ref[:, :blocks], jnp.concatenate(signal, 1).astype(BF16)))
+    x = jnp.concatenate(signal, 1).astype(BF16)
+    s = spectrum([dot(table_ref[i * blocks : (i + 1) * blocks, :blocks], x) for i in range(2)])
 
     real, imag = [], []
     for c in range(2):

time: 60 us -> 59.9 us (level)
  no operation moved by 1% of the time
where the time goes in v8:
time: 59.9 us; the launch traced here: 59.8 us
  blocking collectives  54.4 us (91%)
  Pallas kernels  3.8 us (6%)
  local copies, waits for them, and re-layouts  1.54 us (3%)
    all_to_all x2, blocking collectives, exchange(): return lax.all_to_all(x, AXES, split_axis=0, concat_axis=0, tiled=True)  54.4 us
    unnamed x16, local copies, waits for them, and re-layouts  1.54 us
    pallas_call x1, Pallas kernels, body(): call(conv_kernel, shape((channels, rows), BF16), [vmem((channels, rows),...  1.24 us

profile of v8, /device:TPU:1, one launch (start us, length us, event | category | flops | bytes accessed | tf_op | source)
XLA Modules:
  0.0 59.8 jit_solution(11243700157065755351)
XLA Ops:
  0.0 0.0 copy-start.7
  0.0 0.0 copy-start.5
  0.0 0.0 copy-start.4
  0.0 0.0 copy-start.6
  0.0 0.0 copy-start
  0.0 0.0 copy-start.3
  0.0 0.5 shard_map.82._.twist_ref
  0.5 0.0 copy-start.2
  0.6 0.1 copy-done.7
  0.7 0.2 copy-done.5
  0.9 0.1 copy-done.4
  1.0 0.0 copy-done.6
  1.0 1.1 %copy-done = bf16[1024,1536]{1,0:T(8,128)(2,1)S(1)} copy-done((bf16[1024,1536]{1,0:T(8,128)(2,1)S(1)}, bf16[1024,1536]{1,0:T(8,128)(2,1)}, u32[]{:S(2)}) %copy-start) | copy-done | bytes 3145752
  2.1 0.0 copy-done.3
  2.1 0.0 copy-start.1
  2.1 1.0 %shard_map.83 = (bf16[2048,128]{1,0:T(8,128)(2,1)S(1)}, f32[512,128]{1,0:T(8,128)S(1)}, f32[512,128]{1,0:T(8,128)S(1)}) custom-call(f32[256,256]{1,0:T(8,128)S(1)} %shard_map.82._.twist_ref, bf16[128,1024]{1,0:T(8,128)(2,1)S(1)} %copy-done.3, bf16[1024,1536]{1,0:T(8,128)(2,1)S(1)} %copy-done, f32[3,1536]{1,0:T(4,128)S(1)} %copy-done.6, ...), custom_call_target="tpu_custom_call" | custom-call | tf_op jit(solution)/shard_map/pallas_call | solution.py:188
  3.1 35.4 %all_to_all.16 = bf16[256,8,128]{2,1,0:T(8,128)(2,1)S(1)} all-to-all(bf16[256,8,128]{2,1,0:T(8,128)(2,1)S(1)} %bitcast.6), channel_id=1, replica_groups=mesh['blk'=8,'fft'=32] {'blk','fft'}, dimensions={0} | all-to-all | bytes 1048576 | tf_op jit(solution)/shard_map/all_to_all | solution.py:175
  38.5 0.0 copy-done.2
  38.5 1.2 %shard_map.84 = bf16[512,128]{1,0:T(8,128)(2,1)S(1)} custom-call(bf16[2048,128]{1,0:T(8,128)(2,1)S(1)} %bitcast.5, bf16[512,1024]{1,0:T(8,128)(2,1)S(1)} %copy-done.2, f32[256,256]{1,0:T(8,128)S(1)} %shard_map.82._.twist_ref), custom_call_target="tpu_custom_call" | custom-call | tf_op jit(solution)/shard_map/pallas_call | solution.py:195
  39.8 18.9 %all_to_all.17 = bf16[256,2,128]{2,1,0:T(2,128)(2,1)S(1)} all-to-all(bf16[256,2,128]{2,1,0:T(2,128)(2,1)S(1)} %bitcast.8), channel_id=1, replica_groups=mesh['blk'=8,'fft'=32] {'blk','fft'}, dimensions={0} | all-to-all | bytes 262144 | tf_op jit(solution)/shard_map/all_to_all | solution.py:175
  58.7 0.0 copy-done.1
  58.7 1.1 %shard_map.85 = bf16[128,1024]{1,0:T(8,128)(2,1)} custom-call(bf16[512,128]{1,0:T(8,128)(2,1)S(1)} %bitcast.7, f32[512,128]{1,0:T(8,128)S(1)} %get-tuple-element.9.second_ref, f32[512,128]{1,0:T(8,128)S(1)} %get-tuple-element.10.direct_ref, bf16[512,1024]{1,0:T(8,128)(2,1)S(1)} %copy-done.1), custom_call_target="tpu_custom_call" | custom-call | tf_op jit(solution)/shard_map/pallas_call | solution.py:201
Async XLA Ops:
  0.0 0.7 %copy-start.7 = (f32[512]{0:T(512)S(1)}, f32[512]{0:T(512)}, u32[]{:S(2)}) copy-start(f32[512]{0:T(512)} %param.13) | copy-start | bytes 6148
  0.0 0.9 %copy-start.5 = (bf16[128,512]{1,0:T(8,128)(2,1)S(1)}, bf16[128,512]{1,0:T(8,128)(2,1)}, u32[]{:S(2)}) copy-start(bf16[128,512]{1,0:T(8,128)(2,1)} %anti_ref.1) | copy-start | bytes 393220
  0.0 1.0 %copy-start.4 = (bf16[128,512]{1,0:T(8,128)(2,1)S(1)}, bf16[128,512]{1,0:T(8,128)(2,1)}, u32[]{:S(2)}) copy-start(bf16[128,512]{1,0:T(8,128)(2,1)} %causal_ref.1) | copy-start | bytes 393220
  0.0 1.0 %copy-start.6 = (f32[3,1536]{1,0:T(4,128)S(1)}, f32[3,1536]{1,0:T(4,128)}, u32[]{:S(2)}) copy-start(f32[3,1536]{1,0:T(4,128)} %taps_ref.1) | copy-start | bytes 55300
  0.0 2.1 %copy-start = (bf16[1024,1536]{1,0:T(8,128)(2,1)S(1)}, bf16[1024,1536]{1,0:T(8,128)(2,1)}, u32[]{:S(2)}) copy-start(bf16[1024,1536]{1,0:T(8,128)(2,1)} %w_ref.2) | copy-start | bytes 9437188
  0.0 2.0 %copy-start.3 = (bf16[128,1024]{1,0:T(8,128)(2,1)S(1)}, bf16[128,1024]{1,0:T(8,128)(2,1)}, u32[]{:S(2)}) copy-start(bf16[128,1024]{1,0:T(8,128)(2,1)} %tok_ref.1) | copy-start | bytes 786436
  0.5 38.0 %copy-start.2 = (bf16[512,1024]{1,0:T(8,128)(2,1)S(1)}, bf16[512,1024]{1,0:T(8,128)(2,1)}, u32[]{:S(2)}) copy-start(bf16[512,1024]{1,0:T(8,128)(2,1)} %constant.2.clone.table_ref) | copy-start | bytes 3145732
  2.1 56.6 %copy-start.1 = (bf16[512,1024]{1,0:T(8,128)(2,1)S(1)}, bf16[512,1024]{1,0:T(8,128)(2,1)}, u32[]{:S(2)}) copy-start(bf16[512,1024]{1,0:T(8,128)(2,1)} %w_ref.3) | copy-start | bytes 3145732

commit v9 on v8

--- a/solution.py
+++ b/solution.py
@@ -142,7 +142,12 @@
         real.append(re * cos - im * sin)
         imag.append(re * sin + im * cos)
     e = jnp.concatenate([jnp.concatenate(real, 1), jnp.concatenate(imag, 1)], 0)
-    out = dot(jnp.concatenate([table_ref[:blocks, back], table_ref[blocks : 2 * blocks, back]], 1), e.astype(BF16))
+    e = e.astype(BF16)
+    rows = [
+        jnp.concatenate([table_ref[k : k + tok, back], table_ref[blocks + k : blocks + k + tok, back]], 1)
+        for k in range(0, blocks, tok)
+    ]
+    out = jnp.concatenate([dot(r, e) for r in rows], 0)
     for c in range(2):
         conv = out[:, c * tok : (c + 1) * tok]
         gated = end_second[c] * (conv + end_skip[c] * end_signal[c])

time: 59.9 us -> 59.8 us (level)
  no operation moved by 1% of the time
where the time goes in v9:
time: 59.8 us; the launch traced here: 59.6 us
  blocking collectives  54.4 us (91%)
  Pallas kernels  3.68 us (6%)
  local copies, waits for them, and re-layouts  1.54 us (3%)
    all_to_all x2, blocking collectives, exchange(): return lax.all_to_all(x, AXES, split_axis=0, concat_axis=0, tiled=True)  54.4 us
    unnamed x16, local copies, waits for them, and re-layouts  1.54 us

profile of v9, /device:TPU:1, one launch (start us, length us, event | category | flops | bytes accessed | tf_op | source)
XLA Modules:
  0.0 59.6 jit_solution(14548520480942125714)
XLA Ops:
  0.0 0.0 copy-start.7
  0.0 0.0 copy-start.5
  0.0 0.0 copy-start.4
  0.0 0.0 copy-start.6
  0.0 0.0 copy-start
  0.0 0.0 copy-start.3
  0.0 0.5 shard_map.82._.twist_ref
  0.5 0.0 copy-start.2
  0.6 0.1 copy-done.7
  0.7 0.2 copy-done.5
  0.9 0.1 copy-done.4
  1.0 0.0 copy-done.6
  1.0 1.1 %copy-done = bf16[1024,1536]{1,0:T(8,128)(2,1)S(1)} copy-done((bf16[1024,1536]{1,0:T(8,128)(2,1)S(1)}, bf16[1024,1536]{1,0:T(8,128)(2,1)}, u32[]{:S(2)}) %copy-start) | copy-done | bytes 3145752
  2.1 0.0 copy-done.3
  2.1 0.0 copy-start.1
  2.1 1.0 %shard_map.83 = (bf16[2048,128]{1,0:T(8,128)(2,1)S(1)}, f32[512,128]{1,0:T(8,128)S(1)}, f32[512,128]{1,0:T(8,128)S(1)}) custom-call(f32[256,256]{1,0:T(8,128)S(1)} %shard_map.82._.twist_ref, bf16[128,1024]{1,0:T(8,128)(2,1)S(1)} %copy-done.3, bf16[1024,1536]{1,0:T(8,128)(2,1)S(1)} %copy-done, f32[3,1536]{1,0:T(4,128)S(1)} %copy-done.6, ...), custom_call_target="tpu_custom_call" | custom-call | tf_op jit(solution)/shard_map/pallas_call | solution.py:193
  3.1 35.4 %all_to_all.16 = bf16[256,8,128]{2,1,0:T(8,128)(2,1)S(1)} all-to-all(bf16[256,8,128]{2,1,0:T(8,128)(2,1)S(1)} %bitcast.6), channel_id=1, replica_groups=mesh['blk'=8,'fft'=32] {'blk','fft'}, dimensions={0} | all-to-all | bytes 1048576 | tf_op jit(solution)/shard_map/all_to_all | solution.py:180
  38.5 0.0 copy-done.2
  38.5 1.1 %shard_map.84 = bf16[512,128]{1,0:T(8,128)(2,1)S(1)} custom-call(bf16[2048,128]{1,0:T(8,128)(2,1)S(1)} %bitcast.5, bf16[512,1024]{1,0:T(8,128)(2,1)S(1)} %copy-done.2, f32[256,256]{1,0:T(8,128)S(1)} %shard_map.82._.twist_ref), custom_call_target="tpu_custom_call" | custom-call | tf_op jit(solution)/shard_map/pallas_call | solution.py:200
  39.7 18.9 %all_to_all.17 = bf16[256,2,128]{2,1,0:T(2,128)(2,1)S(1)} all-to-all(bf16[256,2,128]{2,1,0:T(2,128)(2,1)S(1)} %bitcast.8), channel_id=1, replica_groups=mesh['blk'=8,'fft'=32] {'blk','fft'}, dimensions={0} | all-to-all | bytes 262144 | tf_op jit(solution)/shard_map/all_to_all | solution.py:180
  58.6 0.0 copy-done.1
  58.6 1.1 %shard_map.85 = bf16[128,1024]{1,0:T(8,128)(2,1)} custom-call(bf16[512,128]{1,0:T(8,128)(2,1)S(1)} %bitcast.7, f32[512,128]{1,0:T(8,128)S(1)} %get-tuple-element.9.second_ref, f32[512,128]{1,0:T(8,128)S(1)} %get-tuple-element.10.direct_ref, bf16[512,1024]{1,0:T(8,128)(2,1)S(1)} %copy-done.1), custom_call_target="tpu_custom_call" | custom-call | tf_op jit(solution)/shard_map/pallas_call | solution.py:206
Async XLA Ops:
  0.0 0.7 %copy-start.7 = (f32[512]{0:T(512)S(1)}, f32[512]{0:T(512)}, u32[]{:S(2)}) copy-start(f32[512]{0:T(512)} %param.13) | copy-start | bytes 6148
  0.0 0.9 %copy-start.5 = (bf16[128,512]{1,0:T(8,128)(2,1)S(1)}, bf16[128,512]{1,0:T(8,128)(2,1)}, u32[]{:S(2)}) copy-start(bf16[128,512]{1,0:T(8,128)(2,1)} %anti_ref.1) | copy-start | bytes 393220
  0.0 1.0 %copy-start.4 = (bf16[128,512]{1,0:T(8,128)(2,1)S(1)}, bf16[128,512]{1,0:T(8,128)(2,1)}, u32[]{:S(2)}) copy-start(bf16[128,512]{1,0:T(8,128)(2,1)} %causal_ref.1) | copy-start | bytes 393220
  0.0 1.0 %copy-start.6 = (f32[3,1536]{1,0:T(4,128)S(1)}, f32[3,1536]{1,0:T(4,128)}, u32[]{:S(2)}) copy-start(f32[3,1536]{1,0:T(4,128)} %taps_ref.1) | copy-start | bytes 55300
  0.0 2.1 %copy-start = (bf16[1024,1536]{1,0:T(8,128)(2,1)S(1)}, bf16[1024,1536]{1,0:T(8,128)(2,1)}, u32[]{:S(2)}) copy-start(bf16[1024,1536]{1,0:T(8,128)(2,1)} %w_ref.2) | copy-start | bytes 9437188
  0.0 2.0 %copy-start.3 = (bf16[128,1024]{1,0:T(8,128)(2,1)S(1)}, bf16[128,1024]{1,0:T(8,128)(2,1)}, u32[]{:S(2)}) copy-start(bf16[128,1024]{1,0:T(8,128)(2,1)} %tok_ref.1) | copy-start | bytes 786436
  0.5 38.0 %copy-start.2 = (bf16[512,1024]{1,0:T(8,128)(2,1)S(1)}, bf16[512,1024]{1,0:T(8,128)(2,1)}, u32[]{:S(2)}) copy-start(bf16[512,1024]{1,0:T(8,128)(2,1)} %constant.2.clone.table_ref) | copy-start | bytes 3145732
  2.1 56.5 %copy-start.1 = (bf16[512,1024]{1,0:T(8,128)(2,1)S(1)}, bf16[512,1024]{1,0:T(8,128)(2,1)}, u32[]{:S(2)}) copy-start(bf16[512,1024]{1,0:T(8,128)(2,1)} %w_ref.3) | copy-start | bytes 3145732

commit v10 on v6

--- a/solution.py
+++ b/solution.py
@@ -140,7 +140,12 @@
         real.append(re * cos - im * sin)
         imag.append(re * sin + im * cos)
     e = jnp.concatenate([jnp.concatenate(real, 1), jnp.concatenate(imag, 1)], 0)
-    out = dot(jnp.concatenate([table_ref[:blocks, back], table_ref[blocks : 2 * blocks, back]], 1), e.astype(BF16))
+    e = e.astype(BF16)
+    rows = [
+        jnp.concatenate([table_ref[k : k + tok, back], table_ref[blocks + k : blocks + k + tok, back]], 1)
+        for k in range(0, blocks, tok)
+    ]
+    out = jnp.concatenate([dot(r, e) for r in rows], 0)
     for c in range(2):
         conv = out[:, c * tok : (c + 1) * tok]
         gated = end_second[c] * (conv + end_skip[c] * end_signal[c])

time: 60 us -> 60 us (level)
  no operation moved by 1% of the time
where the time goes in v10:
time: 60 us; the launch traced here: 59.8 us
  blocking collectives  54.4 us (91%)
  Pallas kernels  3.87 us (6%)
  local copies, waits for them, and re-layouts  1.54 us (3%)
    all_to_all x2, blocking collectives, exchange(): return lax.all_to_all(x, AXES, split_axis=0, concat_axis=0, tiled=True)  54.4 us
    unnamed x16, local copies, waits for them, and re-layouts  1.54 us
    pallas_call x1, Pallas kernels, body(): call(conv_kernel, shape((channels, rows), BF16), [vmem((channels, rows),...  1.31 us

profile of v10, /device:TPU:1, one launch (start us, length us, event | category | flops | bytes accessed | tf_op | source)
XLA Modules:
  0.0 59.8 jit_solution(306294848312837999)
XLA Ops:
  0.0 0.0 copy-start.7
  0.0 0.0 copy-start.5
  0.0 0.0 copy-start.4
  0.0 0.0 copy-start.6
  0.0 0.0 copy-start
  0.0 0.0 copy-start.3
  0.0 0.5 shard_map.82._.twist_ref
  0.5 0.0 copy-start.2
  0.6 0.1 copy-done.7
  0.7 0.2 copy-done.5
  0.9 0.1 copy-done.4
  1.0 0.0 copy-done.6
  1.0 1.1 %copy-done = bf16[1024,1536]{1,0:T(8,128)(2,1)S(1)} copy-done((bf16[1024,1536]{1,0:T(8,128)(2,1)S(1)}, bf16[1024,1536]{1,0:T(8,128)(2,1)}, u32[]{:S(2)}) %copy-start) | copy-done | bytes 3145752
  2.1 0.0 copy-done.3
  2.1 0.0 copy-start.1
  2.1 1.0 %shard_map.83 = (bf16[2048,128]{1,0:T(8,128)(2,1)S(1)}, f32[512,128]{1,0:T(8,128)S(1)}, f32[512,128]{1,0:T(8,128)S(1)}) custom-call(f32[256,256]{1,0:T(8,128)S(1)} %shard_map.82._.twist_ref, bf16[128,1024]{1,0:T(8,128)(2,1)S(1)} %copy-done.3, bf16[1024,1536]{1,0:T(8,128)(2,1)S(1)} %copy-done, f32[3,1536]{1,0:T(4,128)S(1)} %copy-done.6, ...), custom_call_target="tpu_custom_call" | custom-call | tf_op jit(solution)/shard_map/pallas_call | solution.py:191
  3.1 35.4 %all_to_all.16 = bf16[256,8,128]{2,1,0:T(8,128)(2,1)S(1)} all-to-all(bf16[256,8,128]{2,1,0:T(8,128)(2,1)S(1)} %bitcast.6), channel_id=1, replica_groups=mesh['blk'=8,'fft'=32] {'blk','fft'}, dimensions={0} | all-to-all | bytes 1048576 | tf_op jit(solution)/shard_map/all_to_all | solution.py:178
  38.5 0.0 copy-done.2
  38.5 1.3 %shard_map.84 = bf16[512,128]{1,0:T(8,128)(2,1)S(1)} custom-call(bf16[2048,128]{1,0:T(8,128)(2,1)S(1)} %bitcast.5, bf16[512,1024]{1,0:T(8,128)(2,1)S(1)} %copy-done.2, f32[256,256]{1,0:T(8,128)S(1)} %shard_map.82._.twist_ref), custom_call_target="tpu_custom_call" | custom-call | tf_op jit(solution)/shard_map/pallas_call | solution.py:198
  39.9 18.9 %all_to_all.17 = bf16[256,2,128]{2,1,0:T(2,128)(2,1)S(1)} all-to-all(bf16[256,2,128]{2,1,0:T(2,128)(2,1)S(1)} %bitcast.8), channel_id=1, replica_groups=mesh['blk'=8,'fft'=32] {'blk','fft'}, dimensions={0} | all-to-all | bytes 262144 | tf_op jit(solution)/shard_map/all_to_all | solution.py:178
  58.8 0.0 copy-done.1
  58.8 1.1 %shard_map.85 = bf16[128,1024]{1,0:T(8,128)(2,1)} custom-call(bf16[512,128]{1,0:T(8,128)(2,1)S(1)} %bitcast.7, f32[512,128]{1,0:T(8,128)S(1)} %get-tuple-element.9.second_ref, f32[512,128]{1,0:T(8,128)S(1)} %get-tuple-element.10.direct_ref, bf16[512,1024]{1,0:T(8,128)(2,1)S(1)} %copy-done.1), custom_call_target="tpu_custom_call" | custom-call | tf_op jit(solution)/shard_map/pallas_call | solution.py:204
Async XLA Ops:
  0.0 0.7 %copy-start.7 = (f32[512]{0:T(512)S(1)}, f32[512]{0:T(512)}, u32[]{:S(2)}) copy-start(f32[512]{0:T(512)} %param.13) | copy-start | bytes 6148
  0.0 0.9 %copy-start.5 = (bf16[128,512]{1,0:T(8,128)(2,1)S(1)}, bf16[128,512]{1,0:T(8,128)(2,1)}, u32[]{:S(2)}) copy-start(bf16[128,512]{1,0:T(8,128)(2,1)} %anti_ref.1) | copy-start | bytes 393220
  0.0 1.0 %copy-start.4 = (bf16[128,512]{1,0:T(8,128)(2,1)S(1)}, bf16[128,512]{1,0:T(8,128)(2,1)}, u32[]{:S(2)}) copy-start(bf16[128,512]{1,0:T(8,128)(2,1)} %causal_ref.1) | copy-start | bytes 393220
  0.0 1.0 %copy-start.6 = (f32[3,1536]{1,0:T(4,128)S(1)}, f32[3,1536]{1,0:T(4,128)}, u32[]{:S(2)}) copy-start(f32[3,1536]{1,0:T(4,128)} %taps_ref.1) | copy-start | bytes 55300
  0.0 2.1 %copy-start = (bf16[1024,1536]{1,0:T(8,128)(2,1)S(1)}, bf16[1024,1536]{1,0:T(8,128)(2,1)}, u32[]{:S(2)}) copy-start(bf16[1024,1536]{1,0:T(8,128)(2,1)} %w_ref.2) | copy-start | bytes 9437188
  0.0 2.0 %copy-start.3 = (bf16[128,1024]{1,0:T(8,128)(2,1)S(1)}, bf16[128,1024]{1,0:T(8,128)(2,1)}, u32[]{:S(2)}) copy-start(bf16[128,1024]{1,0:T(8,128)(2,1)} %tok_ref.1) | copy-start | bytes 786436
  0.5 38.0 %copy-start.2 = (bf16[512,1024]{1,0:T(8,128)(2,1)S(1)}, bf16[512,1024]{1,0:T(8,128)(2,1)}, u32[]{:S(2)}) copy-start(bf16[512,1024]{1,0:T(8,128)(2,1)} %constant.2.clone.table_ref) | copy-start | bytes 3145732
  2.1 56.7 %copy-start.1 = (bf16[512,1024]{1,0:T(8,128)(2,1)S(1)}, bf16[512,1024]{1,0:T(8,128)(2,1)}, u32[]{:S(2)}) copy-start(bf16[512,1024]{1,0:T(8,128)(2,1)} %w_ref.3) | copy-start | bytes 3145732
